TPU v7x, 32 devices: a whole 2x2x4 slice. The times are simulated.
32 devices in a mesh: ctx: 4 (over x, core), fsdp: 8 (over z, y).
Axes of the slice: x: 2, y: 2, z: 4, core: 2. Of those that a mesh axis runs over, the one named last changes fastest.
Arguments:
- tokens: bfloat16 [8, 2048, 768], P('fsdp', 'ctx'), may hold values from -6 to 6
- segments: int32 [8, 2048], P('fsdp', 'ctx'), may hold values from 0 to 3, as said below
- padding: int32 [8, 2048], P('fsdp', 'ctx'), may hold values from 0 to 1, as said below
- w_query: bfloat16 [768, 768], P('fsdp'), may hold values from -0.21875 to 0.21875
- w_key: bfloat16 [768, 768], P('fsdp'), may hold values from -0.21875 to 0.21875
- w_value: bfloat16 [768, 768], P('fsdp'), may hold values from -0.21875 to 0.21875
- w_out: bfloat16 [768, 768], P('fsdp'), may hold values from -1.25 to 1.25
- w_up: bfloat16 [768, 3072], P('fsdp'), may hold values from -0.21875 to 0.21875
- w_gate: bfloat16 [768, 3072], P('fsdp'), may hold values from -0.21875 to 0.21875
- w_down: bfloat16 [3072, 768], P('fsdp'), may hold values from -0.109375 to 0.109375
- bias_query: bfloat16 [768], P('fsdp'), may hold values from -3 to 3
- bias_value: bfloat16 [768], P('fsdp'), may hold values from -3 to 3
- bias_out: bfloat16 [768], P('fsdp'), may hold values from -3 to 3
- bias_down: bfloat16 [768], P('fsdp'), may hold values from -3 to 3
- gain_attn: bfloat16 [768], P('fsdp'), may hold values from 0.25 to 1.75
- shift_attn: bfloat16 [768], P('fsdp'), may hold values from -3 to 3
- gain_ffn: bfloat16 [768], P('fsdp'), may hold values from 0.25 to 1.75
- shift_ffn: bfloat16 [768], P('fsdp'), may hold values from -3 to 3
- cotangent: bfloat16 [8, 2048, 768], P('fsdp', 'ctx'), may hold values from -6 to 6
Outputs:
- layer_out: bfloat16 [8, 2048, 768], P('fsdp', 'ctx')
- grad_tokens: float32 [8, 2048, 768], P('fsdp', 'ctx')
- grad_w_query: float32 [768, 768], P('fsdp')
- grad_w_key: float32 [768, 768], P('fsdp')
- grad_w_value: float32 [768, 768], P('fsdp')
- grad_w_out: float32 [768, 768], P('fsdp')
- grad_w_up: float32 [768, 3072], P('fsdp')
- grad_w_gate: float32 [768, 3072], P('fsdp')
- grad_w_down: float32 [3072, 768], P('fsdp')
- grad_bias_query: float32 [768], P('fsdp')
- grad_bias_value: float32 [768], P('fsdp')
- grad_bias_out: float32 [768], P('fsdp')
- grad_bias_down: float32 [768], P('fsdp')
- grad_gain_attn: float32 [768], P('fsdp')
- grad_shift_attn: float32 [768], P('fsdp')
- grad_gain_ffn: float32 [768], P('fsdp')
- grad_shift_ffn: float32 [768], P('fsdp')
Inputs may be any that keep to these rules, and one draw needn't show every extreme that they name: `segments`: along each sequence the document numbers never fall, start at 0 and rise by one where a new document begins. The padding tokens of a sequence form one run at its end.
All inputs are finite; a program needn't handle non-finite values.
Results may differ from a plain program's by a relative error of at most 0.02.
Values may be sent and summed in bfloat16 or wider, within the bound.
No kernel may reach another device: no remote copies, remote signals or barrier semaphores. Data moves between devices by JAX's collectives and lax.ppermute only.
A program may use at most 192 MiB of HBM per device.

v0:
```python
import math

import jax
import jax.numpy as jnp
from jax import lax
from jax.sharding import PartitionSpec as P

H = 12
HD = 64
FF = 3072
HALF = 512


EPSILON = 1e-06
EXCLUDED = -1e30


def extended(block, sides, width):
    for axis, dim in sides:
        count = lax.axis_size(axis)
        forward = [(i, i + 1) for i in range(count - 1)]
        backward = [(target, source) for source, target in forward]
        low = lax.ppermute(
            lax.slice_in_dim(block, block.shape[dim] - width, None, axis=dim), axis, forward
        )
        high = lax.ppermute(lax.slice_in_dim(block, 0, width, axis=dim), axis, backward)
        block = jnp.concatenate([low, block, high], axis=dim)
    return block


def shifted(x, axis, by):
    peers = lax.axis_size(axis)
    pairs = [(i, i + by) for i in range(peers) if 0 <= i + by < peers]
    return lax.ppermute(x, axis, pairs)


def head_slopes(number):
    power_two = 2 ** int(math.floor(math.log2(number)))
    first_part = [2.0 ** (-8.0 * (position + 1) / power_two) for position in range(power_two)]
    extra_part = [
        2.0 ** (-8.0 * (2 * position + 1) / (2 * power_two))
        for position in range(number - power_two)
    ]
    return jnp.array(first_part + extra_part, dtype=jnp.float32)


def norm_parts(values, gain_vec, offset):
    centred = values - jnp.mean(values, axis=-1, keepdims=True)
    variance = jnp.mean(centred * centred, axis=-1, keepdims=True)
    inverse = lax.rsqrt(variance + EPSILON)
    normed = centred * inverse
    return (normed * gain_vec + offset, normed, inverse)


def norm_back(upstream, normed, inverse, gain_vec):
    scaled = upstream * gain_vec
    row_inner = (
        scaled
        - jnp.mean(scaled, axis=-1, keepdims=True)
        - normed * jnp.mean(scaled * normed, axis=-1, keepdims=True)
    )
    return (row_inner * inverse, jnp.sum(upstream * normed, axis=0), jnp.sum(upstream, axis=0))


def gelu_product(gate_value, up_value):
    return jax.nn.gelu(gate_value, approximate=False) * up_value


def contract_rows(left_matrix, right_matrix):
    return lax.dot_general(
        left_matrix, right_matrix, (((0,), (0,)), ((), ())), preferred_element_type=jnp.float32
    )


def contract_cols(left_matrix, right_matrix):
    return lax.dot_general(
        left_matrix, right_matrix, (((1,), (1,)), ((), ())), preferred_element_type=jnp.float32
    )


def on_device(
    tokens,
    segments,
    padding,
    w_query,
    w_key,
    w_value,
    w_out,
    w_up,
    w_gate,
    w_down,
    bias_query,
    bias_value,
    bias_out,
    bias_down,
    gain_attn,
    shift_attn,
    gain_ffn,
    shift_ffn,
    cotangent,
):
    inputs = tokens[0]
    local_rows = inputs.shape[0]
    model_width = inputs.shape[1]
    segment_rows = segments[0]
    key_tags = jnp.where(padding[0] == 1, -1, segment_rows)
    key_span = local_rows + 2 * HALF
    tags_ext = extended(key_tags + 2, (("ctx", 0),), HALF) - 2
    gathered = (
        lax.all_gather(w_query, "fsdp", axis=0, tiled=True),
        lax.all_gather(w_key, "fsdp", axis=0, tiled=True),
        lax.all_gather(w_value, "fsdp", axis=0, tiled=True),
        lax.all_gather(w_out, "fsdp", axis=0, tiled=True),
        lax.all_gather(w_up, "fsdp", axis=0, tiled=True),
        lax.all_gather(w_gate, "fsdp", axis=0, tiled=True),
        lax.all_gather(w_down, "fsdp", axis=0, tiled=True),
        lax.all_gather(bias_query, "fsdp", axis=0, tiled=True),
        lax.all_gather(bias_value, "fsdp", axis=0, tiled=True),
        lax.all_gather(bias_out, "fsdp", axis=0, tiled=True),
        lax.all_gather(bias_down, "fsdp", axis=0, tiled=True),
        lax.all_gather(gain_attn, "fsdp", axis=0, tiled=True),
        lax.all_gather(shift_attn, "fsdp", axis=0, tiled=True),
        lax.all_gather(gain_ffn, "fsdp", axis=0, tiled=True),
        lax.all_gather(shift_ffn, "fsdp", axis=0, tiled=True),
    )
    full_query, full_key, full_value, full_out, full_up, full_gate, full_down = gathered[:7]
    query_bias, value_bias, out_bias, down_bias, attn_gain, attn_shift, ffn_gain, ffn_shift = [
        member.astype(jnp.float32) for member in gathered[7:]
    ]
    full_qkv = jnp.concatenate((full_query, full_key, full_value), axis=1)
    projected = jnp.dot(inputs, full_qkv, preferred_element_type=jnp.float32)
    queries = (projected[:, :model_width] + query_bias).astype(jnp.bfloat16)
    keys_values = jnp.concatenate(
        (projected[:, model_width : 2 * model_width], projected[:, 2 * model_width :] + value_bias),
        axis=1,
    ).astype(jnp.bfloat16)
    edges = extended(keys_values, (("ctx", 0),), HALF)
    keys_ext = edges[:, :model_width]
    values_ext = edges[:, model_width:]
    distance = jnp.abs(
        jnp.arange(local_rows, dtype=jnp.int32)[:, None]
        + HALF
        - jnp.arange(key_span, dtype=jnp.int32)[None, :]
    )
    allowed = (distance <= HALF) & (tags_ext[None, :] == segment_rows[:, None]) | (distance == 0)
    distance_float = distance.astype(jnp.float32)
    score_scale = 1.0 / math.sqrt(HD)
    head_ids = jnp.arange(H, dtype=jnp.int32)
    slopes = head_slopes(H)

    def head_scores(head_index, head_slope):
        query_head = lax.dynamic_slice_in_dim(queries, head_index * HD, HD, 1)
        key_head = lax.dynamic_slice_in_dim(keys_ext, head_index * HD, HD, 1)
        raw_scores = contract_cols(query_head, key_head) * score_scale - head_slope * distance_float
        return (jnp.where(allowed, raw_scores, EXCLUDED), query_head, key_head)

    def forward_head(head_items):
        head_index, head_slope = head_items
        scores, query_head, key_head = head_scores(head_index, head_slope)
        largest = jnp.max(scores, axis=-1, keepdims=True)
        weights = jnp.exp(scores - largest)
        row_totals = jnp.sum(weights, axis=-1, keepdims=True)
        probabilities = (weights / row_totals).astype(jnp.bfloat16)
        value_head = lax.dynamic_slice_in_dim(values_ext, head_index * HD, HD, 1)
        return (
            jnp.dot(probabilities, value_head, preferred_element_type=jnp.float32),
            (largest + jnp.log(row_totals))[:, 0],
        )

    head_mixed, log_totals = lax.map(forward_head, (head_ids, slopes))
    attended = (
        jnp.transpose(head_mixed, (1, 0, 2)).reshape(local_rows, model_width).astype(jnp.bfloat16)
    )
    attn_branch = jnp.dot(attended, full_out, preferred_element_type=jnp.float32) + out_bias
    first_norm, first_normed, first_inverse = norm_parts(
        inputs.astype(jnp.float32) + attn_branch, attn_gain, attn_shift
    )
    normed_low = first_norm.astype(jnp.bfloat16)
    block_rows = math.gcd(local_rows, 512)
    block_count = local_rows // block_rows

    def ffn_forward(normed_block):
        up_value = jnp.dot(normed_block, full_up, preferred_element_type=jnp.float32)
        gate_value = jnp.dot(normed_block, full_gate, preferred_element_type=jnp.float32)
        hidden_block = gelu_product(gate_value, up_value).astype(jnp.bfloat16)
        return (hidden_block, jnp.dot(hidden_block, full_down, preferred_element_type=jnp.float32))

    hidden_blocks, ffn_blocks = lax.map(
        ffn_forward, normed_low.reshape(block_count, block_rows, model_width)
    )
    hidden = hidden_blocks.reshape(local_rows, FF)
    ffn_branch = ffn_blocks.reshape(local_rows, model_width) + down_bias
    output_value, second_normed, second_inverse = norm_parts(
        first_norm + ffn_branch, ffn_gain, ffn_shift
    )
    layer_out = output_value.astype(jnp.bfloat16)
    regathered = (
        lax.all_gather(w_query, "fsdp", axis=0, tiled=True),
        lax.all_gather(w_key, "fsdp", axis=0, tiled=True),
        lax.all_gather(w_value, "fsdp", axis=0, tiled=True),
        lax.all_gather(w_out, "fsdp", axis=0, tiled=True),
        lax.all_gather(w_up, "fsdp", axis=0, tiled=True),
        lax.all_gather(w_gate, "fsdp", axis=0, tiled=True),
        lax.all_gather(w_down, "fsdp", axis=0, tiled=True),
        lax.all_gather(gain_attn, "fsdp", axis=0, tiled=True),
        lax.all_gather(gain_ffn, "fsdp", axis=0, tiled=True),
    )
    back_qkv = jnp.concatenate((regathered[0], regathered[1], regathered[2]), axis=1)
    back_out, back_up, back_gate, back_down = (
        regathered[3],
        regathered[4],
        regathered[5],
        regathered[6],
    )
    back_attn_gain = regathered[7].astype(jnp.float32)
    back_ffn_gain = regathered[8].astype(jnp.float32)
    upstream = cotangent[0].astype(jnp.float32)
    grad_second, grad_ffn_gain, grad_ffn_shift = norm_back(
        upstream, second_normed, second_inverse, back_ffn_gain
    )
    grad_down_bias = jnp.sum(grad_second, axis=0)
    grad_branch = grad_second.astype(jnp.bfloat16)
    grad_w_down = contract_rows(hidden, grad_branch)

    def ffn_back(block_items):
        normed_block, branch_block = block_items
        up_value = jnp.dot(normed_block, back_up, preferred_element_type=jnp.float32)
        gate_value = jnp.dot(normed_block, back_gate, preferred_element_type=jnp.float32)
        hidden_grad = contract_cols(branch_block, back_down)
        unused_value, pullback = jax.vjp(gelu_product, gate_value, up_value)
        grad_gate_block, grad_up_block = pullback(hidden_grad)
        grad_gate_block = grad_gate_block.astype(jnp.bfloat16)
        grad_up_block = grad_up_block.astype(jnp.bfloat16)
        return (
            grad_up_block,
            grad_gate_block,
            contract_cols(grad_up_block, back_up) + contract_cols(grad_gate_block, back_gate),
        )

    up_blocks, gate_blocks, normed_grad_blocks = lax.map(
        ffn_back,
        (
            normed_low.reshape(block_count, block_rows, model_width),
            grad_branch.reshape(block_count, block_rows, model_width),
        ),
    )
    grad_up = up_blocks.reshape(local_rows, FF)
    grad_gate = gate_blocks.reshape(local_rows, FF)
    grad_w_up = contract_rows(normed_low, grad_up)
    grad_w_gate = contract_rows(normed_low, grad_gate)
    grad_normed = grad_second + normed_grad_blocks.reshape(local_rows, model_width)
    grad_first, grad_attn_gain, grad_attn_shift = norm_back(
        grad_normed, first_normed, first_inverse, back_attn_gain
    )
    grad_out_bias = jnp.sum(grad_first, axis=0)
    grad_attn_low = grad_first.astype(jnp.bfloat16)
    grad_w_out = contract_rows(attended, grad_attn_low)
    grad_attended = contract_cols(grad_attn_low, back_out).astype(jnp.bfloat16)
    grad_heads = jnp.transpose(grad_attended.reshape(local_rows, H, HD), (1, 0, 2))

    def backward_head(head_items):
        head_index, head_slope, grad_head, log_total = head_items
        scores, query_head, key_head = head_scores(head_index, head_slope)
        probabilities = jnp.exp(scores - log_total[:, None])
        value_head = lax.dynamic_slice_in_dim(values_ext, head_index * HD, HD, 1)
        grad_probs = contract_cols(grad_head, value_head)
        row_inner = jnp.sum(probabilities * grad_probs, axis=-1, keepdims=True)
        grad_scores = (probabilities * (grad_probs - row_inner)).astype(jnp.bfloat16)
        grad_query = (
            jnp.dot(grad_scores, key_head, preferred_element_type=jnp.float32) * score_scale
        )
        grad_key = contract_rows(grad_scores, query_head) * score_scale
        grad_value = contract_rows(probabilities.astype(jnp.bfloat16), grad_head)
        return (grad_query, grad_key, grad_value)

    query_parts, key_parts, value_parts = lax.map(
        backward_head, (head_ids, slopes, grad_heads, log_totals)
    )
    grad_queries = jnp.transpose(query_parts, (1, 0, 2)).reshape(local_rows, model_width)
    edge_grads = jnp.concatenate(
        (
            jnp.transpose(key_parts, (1, 0, 2)).reshape(key_span, model_width),
            jnp.transpose(value_parts, (1, 0, 2)).reshape(key_span, model_width),
        ),
        axis=1,
    )
    from_next = shifted(edge_grads[:HALF].astype(jnp.bfloat16), "ctx", -1).astype(jnp.float32)
    from_previous = shifted(edge_grads[HALF + local_rows :].astype(jnp.bfloat16), "ctx", 1).astype(
        jnp.float32
    )
    centre_grads = edge_grads[HALF : HALF + local_rows]
    centre_grads = centre_grads + from_next + from_previous
    grad_qkv = jnp.concatenate(
        (grad_queries.astype(jnp.bfloat16), centre_grads.astype(jnp.bfloat16)), axis=1
    )
    grad_w_qkv = contract_rows(inputs, grad_qkv)
    grad_w_query = grad_w_qkv[:, :model_width]
    grad_w_key = grad_w_qkv[:, model_width : 2 * model_width]
    grad_w_value = grad_w_qkv[:, 2 * model_width :]
    grad_query_bias = jnp.sum(grad_qkv[:, :model_width].astype(jnp.float32), axis=0)
    grad_value_bias = jnp.sum(grad_qkv[:, 2 * model_width :].astype(jnp.float32), axis=0)
    grad_inputs = grad_first + contract_cols(grad_qkv, back_qkv)
    shards = (
        lax.psum_scatter(
            grad_w_query.astype(jnp.bfloat16), "fsdp", scatter_dimension=0, tiled=True
        ).astype(jnp.float32),
        lax.psum_scatter(
            grad_w_key.astype(jnp.bfloat16), "fsdp", scatter_dimension=0, tiled=True
        ).astype(jnp.float32),
        lax.psum_scatter(
            grad_w_value.astype(jnp.bfloat16), "fsdp", scatter_dimension=0, tiled=True
        ).astype(jnp.float32),
        lax.psum_scatter(
            grad_w_out.astype(jnp.bfloat16), "fsdp", scatter_dimension=0, tiled=True
        ).astype(jnp.float32),
        lax.psum_scatter(
            grad_w_up.astype(jnp.bfloat16), "fsdp", scatter_dimension=0, tiled=True
        ).astype(jnp.float32),
        lax.psum_scatter(
            grad_w_gate.astype(jnp.bfloat16), "fsdp", scatter_dimension=0, tiled=True
        ).astype(jnp.float32),
        lax.psum_scatter(
            grad_w_down.astype(jnp.bfloat16), "fsdp", scatter_dimension=0, tiled=True
        ).astype(jnp.float32),
        lax.psum_scatter(
            grad_query_bias.astype(jnp.bfloat16), "fsdp", scatter_dimension=0, tiled=True
        ).astype(jnp.float32),
        lax.psum_scatter(
            grad_value_bias.astype(jnp.bfloat16), "fsdp", scatter_dimension=0, tiled=True
        ).astype(jnp.float32),
        lax.psum_scatter(
            grad_out_bias.astype(jnp.bfloat16), "fsdp", scatter_dimension=0, tiled=True
        ).astype(jnp.float32),
        lax.psum_scatter(
            grad_down_bias.astype(jnp.bfloat16), "fsdp", scatter_dimension=0, tiled=True
        ).astype(jnp.float32),
        lax.psum_scatter(
            grad_attn_gain.astype(jnp.bfloat16), "fsdp", scatter_dimension=0, tiled=True
        ).astype(jnp.float32),
        lax.psum_scatter(
            grad_attn_shift.astype(jnp.bfloat16), "fsdp", scatter_dimension=0, tiled=True
        ).astype(jnp.float32),
        lax.psum_scatter(
            grad_ffn_gain.astype(jnp.bfloat16), "fsdp", scatter_dimension=0, tiled=True
        ).astype(jnp.float32),
        lax.psum_scatter(
            grad_ffn_shift.astype(jnp.bfloat16), "fsdp", scatter_dimension=0, tiled=True
        ).astype(jnp.float32),
    )
    summed = (
        lax.psum(shards[0].astype(jnp.bfloat16), "ctx").astype(jnp.float32),
        lax.psum(shards[1].astype(jnp.bfloat16), "ctx").astype(jnp.float32),
        lax.psum(shards[2].astype(jnp.bfloat16), "ctx").astype(jnp.float32),
        lax.psum(shards[3].astype(jnp.bfloat16), "ctx").astype(jnp.float32),
        lax.psum(shards[4].astype(jnp.bfloat16), "ctx").astype(jnp.float32),
        lax.psum(shards[5].astype(jnp.bfloat16), "ctx").astype(jnp.float32),
        lax.psum(shards[6].astype(jnp.bfloat16), "ctx").astype(jnp.float32),
        lax.psum(shards[7].astype(jnp.bfloat16), "ctx").astype(jnp.float32),
        lax.psum(shards[8].astype(jnp.bfloat16), "ctx").astype(jnp.float32),
        lax.psum(shards[9].astype(jnp.bfloat16), "ctx").astype(jnp.float32),
        lax.psum(shards[10].astype(jnp.bfloat16), "ctx").astype(jnp.float32),
        lax.psum(shards[11].astype(jnp.bfloat16), "ctx").astype(jnp.float32),
        lax.psum(shards[12].astype(jnp.bfloat16), "ctx").astype(jnp.float32),
        lax.psum(shards[13].astype(jnp.bfloat16), "ctx").astype(jnp.float32),
        lax.psum(shards[14].astype(jnp.bfloat16), "ctx").astype(jnp.float32),
    )
    matrices = summed[:7]
    vectors = summed[7:]
    return (
        layer_out[None],
        grad_inputs[None],
        matrices[0],
        matrices[1],
        matrices[2],
        matrices[3],
        matrices[4],
        matrices[5],
        matrices[6],
        vectors[0],
        vectors[1],
        vectors[2],
        vectors[3],
        vectors[4],
        vectors[5],
        vectors[6],
        vectors[7],
    )


def solution(mesh):
    in_specs = (
        P("fsdp", "ctx", None),
        P("fsdp", "ctx"),
        P("fsdp", "ctx"),
        P("fsdp", None),
        P("fsdp", None),
        P("fsdp", None),
        P("fsdp", None),
        P("fsdp", None),
        P("fsdp", None),
        P("fsdp", None),
        P("fsdp"),
        P("fsdp"),
        P("fsdp"),
        P("fsdp"),
        P("fsdp"),
        P("fsdp"),
        P("fsdp"),
        P("fsdp"),
        P("fsdp", "ctx", None),
    )
    out_specs = (
        P("fsdp", "ctx", None),
        P("fsdp", "ctx", None),
        P("fsdp", None),
        P("fsdp", None),
        P("fsdp", None),
        P("fsdp", None),
        P("fsdp", None),
        P("fsdp", None),
        P("fsdp", None),
        P("fsdp"),
        P("fsdp"),
        P("fsdp"),
        P("fsdp"),
        P("fsdp"),
        P("fsdp"),
        P("fsdp"),
        P("fsdp"),
    )
    return jax.shard_map(
        on_device, mesh=mesh, in_specs=in_specs, out_specs=out_specs, check_vma=False
    )
```

profile of v0, /device:TPU:0, one launch (start us, length us, event | category | flops | bytes accessed | tf_op | source)
XLA Modules:
  0.0 1283.6 jit_solution(10235435184226084251)
XLA Ops:
  19.0 39.3 %all-reduce.17 = (bf16[768]{0:T(1024)(128)(2,1)S(1)}, bf16[768]{0:T(1024)(128)(2,1)S(1)}, bf16[768]{0:T(1024)(128)(2,1)}, bf16[768]{0:T(1024)(128)(2,1)}, bf16[7...) all-reduce(bf16[768]{0:T(1024)(128)(2,1)S(1)} %dynamic-update-slice, ...), channel_id=1, replica_groups=mesh['ctx'=4,'fsdp'=8] {'fsdp'}, use_global_device_ids=true, to_apply=%add | all-reduce | flops 5376 | bytes 21504
  59.7 36.7 %all-gather.10.cloned.1.call-done = bf16[768,768]{1,0:T(8,128)(2,1)} async-done(((bf16[96,768]{1,0:T(8,128)(2,1)}), bf16[768,768]{1,0:T(8,128)(2,1)}) %all-gather.10.cloned.1.call-update) | async-done | bytes 1179664 | tf_op jit(solution)/shard_map/all_gather | solution.py:111
  97.7 40.7 %all-gather.12.cloned.1.call-done = bf16[768,768]{1,0:T(8,128)(2,1)} async-done(((bf16[96,768]{1,0:T(8,128)(2,1)}), bf16[768,768]{1,0:T(8,128)(2,1)}) %all-gather.12.cloned.1.call-update) | async-done | bytes 1179664 | tf_op jit(solution)/shard_map/all_gather | solution.py:112
  159.3 11.9 pad_maximum_fusion.1
  172.9 4.3 copy.59
  180.6 101.9 %while.10 = (s32[]{:T(128)}, bf16[12,512,64]{1,2,0:T(8,128)(2,1)}, f32[12,512]{1,0:T(8,128)S(1)}, s32[12]{0:T(128)S(1)}, bf16[512,768]{1,0:T(8,128)(2,1)}, /*ind...) while((s32[]{:T(128)}, bf16[12,512,64]{1,2,0:T(8,128)(2,1)}, ...), condition=%wide.region_3.4_spmd.clone.clone.clone, body=%wide.region_0.3_spmd.sunk.clone.clone.clone.sunk | while | flops 215481856 | bytes 10518747 | solution.py:170
  285.8 7.0 fusion.101
  292.9 48.3 %all-gather.18.cloned.1.call-done = bf16[768,3072]{1,0:T(8,128)(2,1)} async-done(((bf16[96,3072]{1,0:T(8,128)(2,1)}), bf16[768,3072]{1,0:T(8,128)(2,1)}) %all-gather.18.cloned.1.call-update) | async-done | bytes 4718608 | tf_op jit(solution)/shard_map/all_gather | solution.py:114
  341.2 19.9 %multiply_convert_fusion.2 = (bf16[512,3072]{1,0:T(8,128)(2,1)}, f32[512,3072]{1,0:T(8,128)}, f32[512,3072]{1,0:T(8,128)}) fusion(f32[512,3072]{1,0:T(8,128)} %fusion.101, bf16[512,768]{1,0:T(8,128)(2,1)S(1)} %fusion.78, bf16[768,3072]{1,0:T(8,128)(2,1)} %all-gather.18.cloned.1.call-done), kind=kOutput, calls=%fused_computation.73 | convolution fusion | flops 2519728128 | bytes 27525120 | tf_op jit(solution)/shard_map/while/body/eval_jaxpr/dot_general | solution.py:183
  361.1 60.4 %all-gather.20.cloned.1.call-done = bf16[3072,768]{1,0:T(8,128)(2,1)} async-done(((bf16[384,768]{1,0:T(8,128)(2,1)}), bf16[3072,768]{1,0:T(8,128)(2,1)}) %all-gather.20.cloned.1.call-update) | async-done | bytes 4718608 | tf_op jit(solution)/shard_map/all_gather | solution.py:116
  421.4 6.1 fusion.100
  431.2 11.1 add_convert_fusion
  442.4 6.1 fusion.102
  454.6 155.5 %while.44 = (s32[]{:T(128)}, bf16[12,512,64]{1,2,0:T(8,128)(2,1)S(1)}, f32[12,1536,64]{1,2,0:T(8,128)}, f32[12,1536,64]{1,2,0:T(8,128)}, s32[12]{0:T(128)S(1)}, ...) while((s32[]{:T(128)}, ...), condition=%wide.region_14.15_spmd.clone.clone.clone, body=%wide.region_12.14_spmd.sunk.clone.clone.clone.sunk | while | flops 518389248 | bytes 26108156 | solution.py:276
  510.0 4.0 multiply_reduce_fusion.7
  523.0 4.0 multiply_reduce_fusion.7
  600.7 4.0 multiply_reduce_fusion.7
  610.2 4.6 fusion.56
  638.6 7.2 convolution_convert_fusion
  646.8 6.2 convolution_convert_fusion.2
  653.2 6.2 convolution_convert_fusion.1
  659.5 49.8 %reduce-scatter.22.cloned.1.call-done = bf16[96,768]{1,0:T(8,128)(2,1)} async-done(((bf16[768,768]{1,0:T(8,128)(2,1)}), bf16[96,768]{1,0:T(8,128)(2,1)}) %reduce-scatter.22.cloned.1.call-update) | async-done | bytes 147472
  711.0 64.7 %reduce-scatter.24.cloned.1.call-done = bf16[96,768]{1,0:T(8,128)(2,1)} async-done(((bf16[768,768]{1,0:T(8,128)(2,1)}), bf16[96,768]{1,0:T(8,128)(2,1)}) %reduce-scatter.24.cloned.1.call-update) | async-done | bytes 147472
  777.4 65.4 %reduce-scatter.26.cloned.1.call-done = bf16[96,768]{1,0:T(8,128)(2,1)} async-done(((bf16[768,768]{1,0:T(8,128)(2,1)}), bf16[96,768]{1,0:T(8,128)(2,1)}) %reduce-scatter.26.cloned.1.call-update) | async-done | bytes 147472
  844.5 65.5 %reduce-scatter.14.cloned.1.call-done = bf16[96,768]{1,0:T(8,128)(2,1)} async-done(((bf16[768,768]{1,0:T(8,128)(2,1)}), bf16[96,768]{1,0:T(8,128)(2,1)}) %reduce-scatter.14.cloned.1.call-update) | async-done | bytes 147472 | tf_op jit(solution)/shard_map/reduce_scatter | solution.py:313
  910.0 97.9 %reduce-scatter.20.cloned.1.call-done = bf16[384,768]{1,0:T(8,128)(2,1)} async-done(((bf16[3072,768]{1,0:T(8,128)(2,1)}), bf16[384,768]{1,0:T(8,128)(2,1)}) %reduce-scatter.20.cloned.1.call-update) | async-done | bytes 589840 | tf_op jit(solution)/shard_map/reduce_scatter | solution.py:322
  1008.0 98.8 %reduce-scatter.16.cloned.1.call-done = bf16[96,3072]{1,0:T(8,128)(2,1)} async-done(((bf16[768,3072]{1,0:T(8,128)(2,1)}), bf16[96,3072]{1,0:T(8,128)(2,1)}) %reduce-scatter.16.cloned.1.call-update) | async-done | bytes 589840 | tf_op jit(solution)/shard_map/reduce_scatter | solution.py:316
  1106.8 98.7 %reduce-scatter.18.cloned.1.call-done = bf16[96,3072]{1,0:T(8,128)(2,1)} async-done(((bf16[768,3072]{1,0:T(8,128)(2,1)}), bf16[96,3072]{1,0:T(8,128)(2,1)}) %reduce-scatter.18.cloned.1.call-update) | async-done | bytes 589840 | tf_op jit(solution)/shard_map/reduce_scatter | solution.py:319
  1209.4 35.9 %all-reduce.16 = (bf16[768]{0:T(1024)(128)(2,1)S(1)}, bf16[768]{0:T(1024)(128)(2,1)S(1)}, bf16[768]{0:T(1024)(128)(2,1)S(1)}, bf16[768]{0:T(1024)(128)(2,1)S(1)}...) all-reduce(bf16[768]{0:T(1024)(128)(2,1)S(1)} %dynamic-update-slice, ...), channel_id=1, replica_groups=mesh['ctx'=4,'fsdp'=8] {'fsdp'}, use_global_device_ids=true, to_apply=%add.7 | all-reduce | flops 6912 | bytes 27648
  1246.0 6.3 all-reduce.18
  1257.6 6.0 add_bitcast_fusion
  1263.6 4.5 all-reduce.22.cloned.1.call-done
  (398 shorter events, 329.8 us)
Async XLA Ops:
  7.2 51.1 %all-gather.8.cloned.1.call-start = ((), (), s32[]{:S(2)}) async-start(), calls=%async_computation.7 | async-start | bytes 1327104 | tf_op jit(solution)/shard_map/all_gather | solution.py:110
  7.9 88.4 %all-gather.10.cloned.1.call-start = ((), (), s32[]{:S(2)}) async-start(), calls=%async_computation.8 | async-start | bytes 1327104 | tf_op jit(solution)/shard_map/all_gather | solution.py:111
  8.7 129.7 %all-gather.12.cloned.1.call-start = ((), (), s32[]{:S(2)}) async-start(), calls=%async_computation.9 | async-start | bytes 1327104 | tf_op jit(solution)/shard_map/all_gather | solution.py:112
  9.4 273.1 %all-gather.14.cloned.1.call-start = ((), (), s32[]{:S(2)}) async-start(), calls=%async_computation.10 | async-start | bytes 1327104 | tf_op jit(solution)/shard_map/all_gather | solution.py:113
  10.0 275.9 %all-gather.16.cloned.1.call-start = ((), (), s32[]{:S(2)}) async-start(), calls=%async_computation.11 | async-start | bytes 5308416 | tf_op jit(solution)/shard_map/all_gather | solution.py:115
  10.6 330.6 %all-gather.18.cloned.1.call-start = ((), (), s32[]{:S(2)}) async-start(), calls=%async_computation.12 | async-start | bytes 5308416 | tf_op jit(solution)/shard_map/all_gather | solution.py:114
  11.1 410.3 %all-gather.20.cloned.1.call-start = ((), (), s32[]{:S(2)}) async-start(), calls=%async_computation.13 | async-start | bytes 5308416 | tf_op jit(solution)/shard_map/all_gather | solution.py:116
  144.9 10.9 copy-start.22
  144.9 10.9 copy-start.21
  144.9 10.9 copy-start.20
  146.4 12.8 %collective-permute-start = (bf16[512,1536]{0,1:T(8,128)(2,1)}, bf16[512,1536]{0,1:T(8,128)(2,1)}, u32[]{:S(2)}, u32[]{:S(2)}) collective-permute-start(bf16[512,1536]{0,1:T(8,128)(2,1)} %pad_maximum_fusion.3), channel_id=1, source_target_pairs={{0,8},{8,16},{16,24},{1,9},{9,17},{17,25},{2,10},{10,18},{18,26},{... | collective-permute-start | bytes 4718600 | tf_op jit(solution)/shard_map/ppermute | solution.py:23
  148.9 10.4 collective-permute-start.1
  150.2 5.6 collective-permute-start.2
  153.8 4.3 collective-permute-start.3
  155.2 554.2 %reduce-scatter.22.cloned.1.call-start = ((), (), s32[]{:S(2)}) async-start(), calls=%async_computation.18 | async-start | bytes 1327104
  285.8 55.4 %copy-start.7 = (bf16[512,768]{1,0:T(8,128)(2,1)}, bf16[512,768]{1,0:T(8,128)(2,1)S(1)}, u32[]{:S(2)}) copy-start(bf16[512,768]{1,0:T(8,128)(2,1)S(1)} %fusion.78) | copy-start | bytes 2359300
  428.7 19.8 %slice-start = ((s8[4718592]{0:T(1024)(128)(4,1)}), s8[4194304]{0:T(1024)(128)(4,1)S(1)}, s32[]{:S(2)}) async-start(s8[4718592]{0:T(1024)(128)(4,1)} %bitcast.124), calls=%async_computation.22 | async-start | bytes 8388608
  429.2 13.1 %copy-start.10 = (f32[512,768]{1,0:T(8,128)}, f32[512,768]{1,0:T(8,128)S(1)}, u32[]{:S(2)}) copy-start(f32[512,768]{1,0:T(8,128)S(1)} %get-tuple-element.586) | copy-start | bytes 4718596
  431.2 17.2 %slice-start.1 = ((s8[4718592]{0:T(1024)(128)(4,1)}), s8[524288]{0:T(1024)(128)(4,1)S(1)}, s32[]{:S(2)}) async-start(s8[4718592]{0:T(1024)(128)(4,1)} %bitcast.124), calls=%async_computation.23 | async-start | bytes 1048576
  610.2 15.1 %copy-start.9 = (bf16[12,512,64]{1,2,0:T(8,128)(2,1)}, bf16[12,512,64]{1,2,0:T(8,128)(2,1)S(1)}, u32[]{:S(2)}) copy-start(bf16[12,512,64]{1,2,0:T(8,128)(2,1)S(1)} %get-tuple-element.189) | copy-start | bytes 2359300
  615.0 5.3 collective-permute-start.4
  616.3 6.2 collective-permute-start.5
  630.4 145.3 %reduce-scatter.24.cloned.1.call-start = ((), (), s32[]{:S(2)}) async-start(), calls=%async_computation.19 | async-start | bytes 1327104
  633.0 209.8 %reduce-scatter.26.cloned.1.call-start = ((), (), s32[]{:S(2)}) async-start(), calls=%async_computation.20 | async-start | bytes 1327104
  635.5 274.5 %reduce-scatter.14.cloned.1.call-start = ((), (), s32[]{:S(2)}) async-start(), calls=%async_computation.14 | async-start | bytes 1327104 | tf_op jit(solution)/shard_map/reduce_scatter | solution.py:313
  638.5 369.4 %reduce-scatter.20.cloned.1.call-start = ((), (), s32[]{:S(2)}) async-start(), calls=%async_computation.17 | async-start | bytes 5308416 | tf_op jit(solution)/shard_map/reduce_scatter | solution.py:322
  645.7 461.1 %reduce-scatter.16.cloned.1.call-start = ((), (), s32[]{:S(2)}) async-start(), calls=%async_computation.15 | async-start | bytes 5308416 | tf_op jit(solution)/shard_map/reduce_scatter | solution.py:316
  653.1 552.4 %reduce-scatter.18.cloned.1.call-start = ((), (), s32[]{:S(2)}) async-start(), calls=%async_computation.16 | async-start | bytes 5308416 | tf_op jit(solution)/shard_map/reduce_scatter | solution.py:319
  659.4 546.1 %copy-start.1 = (bf16[1,512,768]{2,1,0:T(8,128)(2,1)S(1)}, bf16[1,512,768]{2,1,0:T(8,128)(2,1)}, u32[]{:S(2)}) copy-start(bf16[1,512,768]{2,1,0:T(8,128)(2,1)} %param.42) | copy-start | bytes 2359300
  659.4 546.3 %copy-start.25 = (bf16[96]{0:T(256)(128)(2,1)S(1)}, bf16[96]{0:T(256)(128)(2,1)}, u32[]{:S(2)}) copy-start(bf16[96]{0:T(256)(128)(2,1)} %param.41) | copy-start | bytes 580
  659.4 608.6 %all-reduce.22.cloned.1.call-start = ((), (), s32[]{:S(2)}) async-start(), calls=%async_computation.21 | async-start | bytes 5013504 | tf_op jit(solution)/shard_map/psum | solution.py:351
  1205.7 51.9 %copy-start.4 = (f32[512,768]{1,0:T(8,128)S(1)}, f32[512,768]{1,0:T(8,128)}, u32[]{:S(2)}) copy-start(f32[512,768]{1,0:T(8,128)} %copy-done.2) | copy-start | bytes 4718596
  (19 other events, 89.4 us)
Sparse Core Ops, SparseCore 0:
  10.2 44.0 all-gather.7
  56.5 39.8 all-gather.9
  98.5 39.8 all-gather.11
  140.4 39.8 all-gather.13
  182.4 78.7 all-gather.15
  263.1 78.0 all-gather.17
  343.4 78.0 all-gather.19
  630.5 78.7 reduce-scatter.21
  712.7 62.9 reduce-scatter.23
  779.5 63.2 reduce-scatter.25
  846.8 63.1 reduce-scatter.13
  913.5 94.3 reduce-scatter.19
  1011.6 95.1 reduce-scatter.15
  1110.3 95.1 reduce-scatter.17
  1208.8 59.1 all-reduce.21
where the time goes:
time: 1290 us; the launch traced here: 1280 us
  waiting for transfers between devices  740 us (57%)
  matrix products  292 us (23%)
  blocking collectives  81.5 us (6%)
  local copies, waits for them, and re-layouts  74.2 us (6%)
  other arithmetic  49.1 us (4%)
  loops' own time  16.3 us (1%)
  between operations  16.2 us (1%)
  starting transfers between devices  14.7 us (1%)
    unnamed x18, waiting for transfers between devices  184 us
    dot_general x41, matrix products, contract_cols(): lax.dot_general(left_matrix, right_matrix, (((1,), (1,)), ((), ())), pref...  137 us
    reduce_scatter x1, waiting for transfers between devices, on_device(): lax.psum_scatter(grad_w_up.astype(jnp.bfloat16), 'fsdp', scatter_dimensio...  98.8 us
    reduce_scatter x1, waiting for transfers between devices, on_device(): lax.psum_scatter(grad_w_gate.astype(jnp.bfloat16), 'fsdp', scatter_dimens...  98.7 us
    reduce_scatter x1, waiting for transfers between devices, on_device(): lax.psum_scatter(grad_w_down.astype(jnp.bfloat16), 'fsdp', scatter_dimens...  97.9 us
    unnamed x2, blocking collectives  75.2 us
    reduce_scatter x1, waiting for transfers between devices, on_device(): lax.psum_scatter(grad_w_out.astype(jnp.bfloat16), 'fsdp', scatter_dimensi...  65.5 us
    dot_general x29, matrix products, contract_rows(): lax.dot_general(left_matrix, right_matrix, (((0,), (0,)), ((), ())), pref...  64.5 us
  transfers between devices with their start and end apart: 21, of which 15 were waited for; matrix products, arithmetic and copies ran while one was open for 16% of the time, Pallas kernels for 0%

commit v1 on v0

v1 whole, which is shorter than its diff:
```python
import math
import jax
import jax.numpy as jnp
from jax import lax
from jax.experimental import pallas as pl
from jax.experimental.pallas import tpu as pltpu
from jax.sharding import PartitionSpec as P

H = 12
HD = 64
FF = 3072
HALF = 512
QB = 256
BIG = 1e30
VMEM_LIMIT = 56 * 1024 * 1024


def dot_nn(a, b):
    return lax.dot_general(a, b, (((1,), (0,)), ((), ())), preferred_element_type=jnp.float32)


def dot_nt(a, b):
    return lax.dot_general(a, b, (((1,), (1,)), ((), ())), preferred_element_type=jnp.float32)


def dot_tn(a, b):
    return lax.dot_general(a, b, (((0,), (0,)), ((), ())), preferred_element_type=jnp.float32)


def fill_distance(dist, seg_ref, tag_ref, span):
    blocks = dist.shape[0]
    for b in range(blocks):
        base = b * QB
        key_pos = lax.broadcasted_iota(jnp.int32, (span, QB), 0)
        row_pos = lax.broadcasted_iota(jnp.int32, (span, QB), 1) + HALF
        gap = jnp.abs(key_pos - row_pos)
        same = tag_ref[base : base + span, :] == seg_ref[:, base : base + QB]
        kept = ((gap <= HALF) & same) | (gap == 0)
        dist[b] = jnp.where(kept, gap.astype(jnp.float32), BIG)


def attn_fwd_kernel(slopes, q_ref, k_ref, v_ref, seg_ref, tag_ref, out_ref, lse_ref, dist):
    rows = q_ref.shape[0]
    span = QB + 2 * HALF
    pair = pl.program_id(0)

    @pl.when(pair == 0)
    def _():
        fill_distance(dist, seg_ref, tag_ref, span)

    lane = lax.broadcasted_iota(jnp.int32, (QB, 2 * HD), 1)
    v_t = v_ref[...].T
    for b in range(rows // QB):
        base = b * QB
        q = q_ref[base : base + QB, :]
        k = k_ref[base : base + span, :]
        parts = []
        for a in range(2):
            mine = (lane >= HD) if a else (lane < HD)
            q_a = jnp.where(mine, q, jnp.zeros_like(q)) * jnp.asarray(1.0 / math.sqrt(HD), q.dtype)
            s = dot_nt(k, q_a) - slopes[2 * pair + a] * dist[b]
            top = jnp.max(s, axis=0, keepdims=True)
            p = jnp.exp(s - top)
            total = jnp.sum(p, axis=0, keepdims=True)
            o_t = dot_nn(v_t[a * HD : (a + 1) * HD, base : base + span], p.astype(jnp.bfloat16))
            parts.append(o_t * (1.0 / total))
            lse_ref[0, a : a + 1, base : base + QB] = top + jnp.log(total)
        out_ref[base : base + QB, :] = jnp.concatenate(parts, axis=0).T.astype(jnp.bfloat16)


def attention_forward(queries, keys, values, seg_row, tag_col, slopes):
    rows, width = queries.shape
    ext = keys.shape[0]
    span = QB + 2 * HALF
    pairs = width // (2 * HD)
    return pl.pallas_call(
        attn_fwd_kernel,
        grid=(pairs,),
        in_specs=[
            pl.BlockSpec(memory_space=pltpu.SMEM),
            pl.BlockSpec((rows, 2 * HD), lambda h: (0, h)),
            pl.BlockSpec((ext, 2 * HD), lambda h: (0, h)),
            pl.BlockSpec((ext, 2 * HD), lambda h: (0, h)),
            pl.BlockSpec((1, rows), lambda h: (0, 0)),
            pl.BlockSpec((ext, 1), lambda h: (0, 0)),
        ],
        out_specs=[
            pl.BlockSpec((rows, 2 * HD), lambda h: (0, h)),
            pl.BlockSpec((1, 8, rows), lambda h: (h, 0, 0)),
        ],
        out_shape=[
            jax.ShapeDtypeStruct((rows, width), jnp.bfloat16),
            jax.ShapeDtypeStruct((pairs, 8, rows), jnp.float32),
        ],
        scratch_shapes=[pltpu.VMEM((rows // QB, span, QB), jnp.float32)],
        compiler_params=pltpu.CompilerParams(vmem_limit_bytes=VMEM_LIMIT),
        cost_estimate=pl.CostEstimate(
            flops=4 * 2 * H * rows * span * HD, bytes_accessed=12 * ext * width, transcendentals=H * rows * span
        ),
    )(slopes, queries, keys, values, seg_row, tag_col)


def attn_bwd_kernel(
    slopes, q_ref, k_ref, v_ref, o_ref, do_ref, lse_ref, seg_ref, tag_ref,
    dq_ref, low_ref, mid_ref, high_ref, dist, dk_acc, dv_acc,
):
    rows = q_ref.shape[0]
    span = QB + 2 * HALF
    pair = pl.program_id(0)

    @pl.when(pair == 0)
    def _():
        fill_distance(dist, seg_ref, tag_ref, span)

    lane = lax.broadcasted_iota(jnp.int32, (QB, 2 * HD), 1)
    lane_one = lax.broadcasted_iota(jnp.int32, (8, 2 * HD), 1)
    k_t = k_ref[...].T
    scale = 1.0 / math.sqrt(HD)
    dk_acc[...] = jnp.zeros_like(dk_acc)
    dv_acc[...] = jnp.zeros_like(dv_acc)
    for b in range(rows // QB):
        base = b * QB
        q = q_ref[base : base + QB, :] * jnp.asarray(scale, jnp.bfloat16)
        do = do_ref[base : base + QB, :]
        k = k_ref[base : base + span, :]
        v = v_ref[base : base + span, :]
        mixed = do.astype(jnp.float32) * o_ref[base : base + QB, :].astype(jnp.float32)
        parts = []
        ps = []
        dss = []
        qs = []
        dos = []
        for a in range(2):
            mine = (lane >= HD) if a else (lane < HD)
            mine_one = (lane_one >= HD) if a else (lane_one < HD)
            q_a = jnp.where(mine, q, jnp.zeros_like(q))
            do_a = jnp.where(mine, do, jnp.zeros_like(do))
            delta = lax.dot_general(
                mine_one.astype(jnp.float32), mixed, (((1,), (1,)), ((), ())),
                preferred_element_type=jnp.float32, precision=lax.Precision.HIGHEST,
            )[0:1]
            s = dot_nt(k, q_a) - slopes[2 * pair + a] * dist[b]
            p = jnp.exp(s - lse_ref[0, a : a + 1, base : base + QB])
            dp = dot_nt(v, do_a)
            ds = (p * (dp - delta)).astype(jnp.bfloat16)
            parts.append(dot_nn(k_t[a * HD : (a + 1) * HD, base : base + span], ds) * scale)
            ps.append(p.astype(jnp.bfloat16))
            dss.append(ds)
            qs.append(q_a)
            dos.append(do_a)
        dq_ref[base : base + QB, :] = jnp.concatenate(parts, axis=0).T.astype(jnp.bfloat16)
        dk_acc[base : base + span, :] += dot_nn(
            jnp.concatenate(dss, axis=1), jnp.concatenate(qs, axis=0)
        )
        dv_acc[base : base + span, :] += dot_nn(
            jnp.concatenate(ps, axis=1), jnp.concatenate(dos, axis=0)
        )
    low_ref[0] = dk_acc[:HALF, :].astype(jnp.bfloat16)
    low_ref[1] = dv_acc[:HALF, :].astype(jnp.bfloat16)
    mid_ref[0] = dk_acc[HALF : HALF + rows, :]
    mid_ref[1] = dv_acc[HALF : HALF + rows, :]
    high_ref[0] = dk_acc[HALF + rows :, :].astype(jnp.bfloat16)
    high_ref[1] = dv_acc[HALF + rows :, :].astype(jnp.bfloat16)


def attention_backward(queries, keys, values, attended, grad_attended, lse, seg_row, tag_col, slopes):
    rows, width = queries.shape
    ext = keys.shape[0]
    span = QB + 2 * HALF
    pairs = width // (2 * HD)
    row_spec = pl.BlockSpec((rows, 2 * HD), lambda h: (0, h))
    ext_spec = pl.BlockSpec((ext, 2 * HD), lambda h: (0, h))
    return pl.pallas_call(
        attn_bwd_kernel,
        grid=(pairs,),
        in_specs=[
            pl.BlockSpec(memory_space=pltpu.SMEM),
            row_spec, ext_spec, ext_spec, row_spec, row_spec,
            pl.BlockSpec((1, 8, rows), lambda h: (h, 0, 0)),
            pl.BlockSpec((1, rows), lambda h: (0, 0)),
            pl.BlockSpec((ext, 1), lambda h: (0, 0)),
        ],
        out_specs=[
            row_spec,
            pl.BlockSpec((2, HALF, 2 * HD), lambda h: (0, 0, h)),
            pl.BlockSpec((2, rows, 2 * HD), lambda h: (0, 0, h)),
            pl.BlockSpec((2, HALF, 2 * HD), lambda h: (0, 0, h)),
        ],
        out_shape=[
            jax.ShapeDtypeStruct((rows, width), jnp.bfloat16),
            jax.ShapeDtypeStruct((2, HALF, width), jnp.bfloat16),
            jax.ShapeDtypeStruct((2, rows, width), jnp.float32),
            jax.ShapeDtypeStruct((2, HALF, width), jnp.bfloat16),
        ],
        scratch_shapes=[
            pltpu.VMEM((rows // QB, span, QB), jnp.float32),
            pltpu.VMEM((ext, 2 * HD), jnp.float32),
            pltpu.VMEM((ext, 2 * HD), jnp.float32),
        ],
        compiler_params=pltpu.CompilerParams(vmem_limit_bytes=VMEM_LIMIT),
        cost_estimate=pl.CostEstimate(
            flops=10 * 2 * H * rows * span * HD, bytes_accessed=20 * ext * width, transcendentals=H * rows * span
        ),
    )(slopes, queries, keys, values, attended, grad_attended, lse, seg_row, tag_col)


EPSILON = 1e-06
VECTORS = 8


def head_slopes(number):
    power_two = 2 ** int(math.floor(math.log2(number)))
    first_part = [2.0 ** (-8.0 * (position + 1) / power_two) for position in range(power_two)]
    extra_part = [
        2.0 ** (-8.0 * (2 * position + 1) / (2 * power_two))
        for position in range(number - power_two)
    ]
    return jnp.array(first_part + extra_part, dtype=jnp.float32)


def from_previous(x):
    count = lax.axis_size("ctx")
    return lax.ppermute(x, "ctx", [(i, i + 1) for i in range(count - 1)])


def from_next(x):
    count = lax.axis_size("ctx")
    return lax.ppermute(x, "ctx", [(i + 1, i) for i in range(count - 1)])


def norm_parts(values, gain_vec, offset):
    centred = values - jnp.mean(values, axis=-1, keepdims=True)
    variance = jnp.mean(centred * centred, axis=-1, keepdims=True)
    inverse = lax.rsqrt(variance + EPSILON)
    normed = centred * inverse
    return (normed * gain_vec + offset, normed, inverse)


def norm_back(upstream, normed, inverse, gain_vec):
    scaled = upstream * gain_vec
    row_inner = (
        scaled
        - jnp.mean(scaled, axis=-1, keepdims=True)
        - normed * jnp.mean(scaled * normed, axis=-1, keepdims=True)
    )
    return (row_inner * inverse, jnp.sum(upstream * normed, axis=0), jnp.sum(upstream, axis=0))


def gelu_product(gate_value, up_value):
    return jax.nn.gelu(gate_value, approximate=False) * up_value


def gather_rows(shard):
    count = lax.axis_size("ctx")
    part = shard.shape[0] // count
    mine = lax.dynamic_slice_in_dim(shard, lax.axis_index("ctx") * part, part, 0)
    return lax.all_gather(mine, ("fsdp", "ctx"), axis=0, tiled=True)


def scatter_rows(full):
    return lax.psum_scatter(
        full.astype(jnp.bfloat16), ("fsdp", "ctx"), scatter_dimension=0, tiled=True
    )


def on_device(
    tokens, segments, padding,
    w_query, w_key, w_value, w_out, w_up, w_gate, w_down,
    bias_query, bias_value, bias_out, bias_down, gain_attn, shift_attn, gain_ffn, shift_ffn,
    cotangent,
):
    inputs = tokens[0]
    rows, width = inputs.shape
    segment_rows = segments[0]
    key_tags = jnp.where(padding[0] == 1, -1, segment_rows)
    tag_low = from_previous(key_tags + 2) - 2
    tag_high = from_next(key_tags + 2) - 2
    tag_col = jnp.concatenate([tag_low, key_tags, tag_high])[:, None]
    seg_row = segment_rows[None, :]
    slopes = head_slopes(H)

    vectors = jnp.stack(
        (bias_query, bias_value, bias_out, bias_down, gain_attn, shift_attn, gain_ffn, shift_ffn), axis=1
    )
    vectors = jnp.pad(vectors, ((0, 0), (0, 128 - VECTORS)))
    full_first = gather_rows(jnp.concatenate((w_query, w_key, w_value, vectors), axis=1))
    full_qkv = full_first[:, : 3 * width]
    vec = full_first[:, 3 * width : 3 * width + VECTORS].T.astype(jnp.float32)
    query_bias, value_bias, out_bias, down_bias, attn_gain, attn_shift, ffn_gain, ffn_shift = [
        vec[i] for i in range(VECTORS)
    ]
    full_mid = gather_rows(jnp.concatenate((w_out, w_up, w_gate), axis=1))
    full_out = full_mid[:, :width]
    full_up_gate = full_mid[:, width:]
    full_down = gather_rows(w_down)

    projected = dot_nn(inputs, full_qkv)
    queries = (projected[:, :width] + query_bias).astype(jnp.bfloat16)
    keys_values = jnp.concatenate(
        (projected[:, width : 2 * width], projected[:, 2 * width :] + value_bias), axis=1
    ).astype(jnp.bfloat16)
    kv_low = from_previous(keys_values[rows - HALF :])
    kv_high = from_next(keys_values[:HALF])
    kv = jnp.concatenate([kv_low, keys_values, kv_high], axis=0)
    keys_ext = kv[:, :width]
    values_ext = kv[:, width:]
    attended, lse = attention_forward(queries, keys_ext, values_ext, seg_row, tag_col, slopes)

    attn_branch = dot_nn(attended, full_out) + out_bias
    first_norm, first_normed, first_inverse = norm_parts(
        inputs.astype(jnp.float32) + attn_branch, attn_gain, attn_shift
    )
    normed_low = first_norm.astype(jnp.bfloat16)
    up_gate = dot_nn(normed_low, full_up_gate)
    up_value = up_gate[:, :FF]
    gate_value = up_gate[:, FF:]
    hidden = gelu_product(gate_value, up_value).astype(jnp.bfloat16)
    ffn_branch = dot_nn(hidden, full_down) + down_bias
    output_value, second_normed, second_inverse = norm_parts(
        first_norm + ffn_branch, ffn_gain, ffn_shift
    )
    layer_out = output_value.astype(jnp.bfloat16)

    upstream = cotangent[0].astype(jnp.float32)
    grad_second, grad_ffn_gain, grad_ffn_shift = norm_back(
        upstream, second_normed, second_inverse, ffn_gain
    )
    grad_down_bias = jnp.sum(grad_second, axis=0)
    grad_branch = grad_second.astype(jnp.bfloat16)
    shard_down = scatter_rows(dot_tn(hidden, grad_branch))

    hidden_grad = dot_nt(grad_branch, full_down)
    unused_value, pullback = jax.vjp(gelu_product, gate_value, up_value)
    grad_gate, grad_up = pullback(hidden_grad)
    grad_up_gate = jnp.concatenate((grad_up, grad_gate), axis=1).astype(jnp.bfloat16)
    shard_up_gate = scatter_rows(dot_tn(normed_low, grad_up_gate))
    grad_normed = grad_second + dot_nt(grad_up_gate, full_up_gate)
    grad_first, grad_attn_gain, grad_attn_shift = norm_back(
        grad_normed, first_normed, first_inverse, attn_gain
    )
    grad_out_bias = jnp.sum(grad_first, axis=0)
    grad_attn_low = grad_first.astype(jnp.bfloat16)
    grad_w_out = dot_tn(attended, grad_attn_low)
    grad_attended = dot_nt(grad_attn_low, full_out).astype(jnp.bfloat16)

    grad_queries, low, mid, high = attention_backward(
        queries, keys_ext, values_ext, attended, grad_attended, lse, seg_row, tag_col, slopes
    )
    centre = mid.at[:, rows - HALF :].add(from_next(low).astype(jnp.float32))
    centre = centre.at[:, :HALF].add(from_previous(high).astype(jnp.float32)).astype(jnp.bfloat16)
    grad_qkv = jnp.concatenate((grad_queries, centre[0], centre[1]), axis=1)
    grad_w_qkv = dot_tn(inputs, grad_qkv)
    grad_query_bias = jnp.sum(grad_queries.astype(jnp.float32), axis=0)
    grad_value_bias = jnp.sum(centre[1].astype(jnp.float32), axis=0)
    grad_vectors = jnp.stack(
        (
            grad_query_bias, grad_value_bias, grad_out_bias, grad_down_bias,
            grad_attn_gain, grad_attn_shift, grad_ffn_gain, grad_ffn_shift,
        ),
        axis=1,
    )
    grad_vectors = jnp.pad(grad_vectors, ((0, 0), (0, 128 - VECTORS)))
    shard_last = scatter_rows(jnp.concatenate((grad_w_qkv, grad_w_out, grad_vectors), axis=1))
    grad_inputs = grad_first + dot_nt(grad_qkv, full_qkv)

    def whole(shard):
        return lax.all_gather(shard, "ctx", axis=0, tiled=True).astype(jnp.float32)

    down = whole(shard_down)
    up_gate_rows = whole(shard_up_gate)
    last = whole(shard_last)
    return (
        layer_out[None],
        grad_inputs[None],
        last[:, :width],
        last[:, width : 2 * width],
        last[:, 2 * width : 3 * width],
        last[:, 3 * width : 4 * width],
        up_gate_rows[:, :FF],
        up_gate_rows[:, FF:],
        down,
    ) + tuple(last[:, 4 * width + i] for i in range(VECTORS))


def solution(mesh):
    rows_spec = P("fsdp", "ctx", None)
    in_specs = (
        (rows_spec, P("fsdp", "ctx"), P("fsdp", "ctx"))
        + (P("fsdp", None),) * 7
        + (P("fsdp"),) * VECTORS
        + (rows_spec,)
    )
    out_specs = (rows_spec, rows_spec) + (P("fsdp", None),) * 7 + (P("fsdp"),) * VECTORS
    return jax.shard_map(
        on_device, mesh=mesh, in_specs=in_specs, out_specs=out_specs, check_vma=False
    )
```

time: 1290 us -> 697 us (0.54)
  waiting for transfers between devices: 740 us -> 458 us
  matrix products: 292 us -> 75.7 us
  blocking collectives: 81.5 us -> 15.2 us
  local copies, waits for them, and re-layouts: 74.2 us -> 19.7 us
  Pallas kernels: 0 us -> 54.2 us
  loops' own time: 16.3 us -> 0 us
    dot_general x99 -> x12, matrix products: 292 us -> 75.7 us  [the longest x4 30.6 us: dot_nt(): lax.dot_general(a, b, (((1,), (1,)), ((), ())), preferred_element_type=jn...]
    reduce_scatter x4 -> x2, waiting for transfers between devices: 361 us -> 164 us  [scatter_rows(): lax.psum_scatter(full.astype(jnp.bfloat16), ('fsdp', 'ctx'), scatter_dime...]
    unnamed x2 -> x0, blocking collectives: 75.2 us -> none
    pallas_call x0 -> x2, Pallas kernels: none -> 54.2 us  [the longest x1 29.9 us: attention_backward(): pl.pallas_call(attn_bwd_kernel, grid=(pairs,), in_specs=[pl.BlockSpec(mem...]
    unnamed x18 -> x8, waiting for transfers between devices: 184 us -> 146 us
    all_gather x7 -> x4, waiting for transfers between devices: 186 us -> 149 us  [the longest x3 139 us: gather_rows(): return lax.all_gather(mine, ('fsdp', 'ctx'), axis=0, tiled=True)]
    unnamed x99 -> x31, local copies, waits for them, and re-layouts: 38.7 us -> 7.63 us
    dynamic_slice x60 -> x1, local copies, waits for them, and re-layouts: 28.3 us -> 0.68 us  [gather_rows(): lax.dynamic_slice_in_dim(shard, lax.axis_index('ctx') * part, part, 0)]
  transfers between devices with their start and end apart: 21 -> 13, of which waited for: 15 -> 8; matrix products, arithmetic and copies ran while one was open for 16% -> 13% of each run, Pallas kernels for 0% -> 8%
where the time goes in v1:
time: 697 us; the launch traced here: 693 us
  waiting for transfers between devices  458 us (66%)
  matrix products  75.7 us (11%)
  Pallas kernels  54.2 us (8%)
  other arithmetic  37.7 us (5%)
  local copies, waits for them, and re-layouts  19.7 us (3%)
  starting transfers between devices  16.4 us (2%)
  between operations  15.5 us (2%)
  blocking collectives  15.2 us (2%)
    reduce_scatter x2, waiting for transfers between devices, scatter_rows(): lax.psum_scatter(full.astype(jnp.bfloat16), ('fsdp', 'ctx'), scatter_dime...  164 us
    unnamed x8, waiting for transfers between devices  146 us
    all_gather x3, waiting for transfers between devices, gather_rows(): return lax.all_gather(mine, ('fsdp', 'ctx'), axis=0, tiled=True)  139 us
    dot_general x4, matrix products, dot_nt(): lax.dot_general(a, b, (((1,), (1,)), ((), ())), preferred_element_type=jn...  30.6 us
    pallas_call x1, Pallas kernels, attention_backward(): pl.pallas_call(attn_bwd_kernel, grid=(pairs,), in_specs=[pl.BlockSpec(mem...  29.9 us
    pallas_call x1, Pallas kernels, attention_forward(): pl.pallas_call(attn_fwd_kernel, grid=(pairs,), in_specs=[pl.BlockSpec(mem...  24.4 us
    dot_general x4, matrix products, dot_tn(): lax.dot_general(a, b, (((0,), (0,)), ((), ())), preferred_element_type=jn...  23.9 us
    dot_general x4, matrix products, dot_nn(): lax.dot_general(a, b, (((1,), (0,)), ((), ())), preferred_element_type=jn...  21.2 us
  transfers between devices with their start and end apart: 13, of which 8 were waited for; matrix products, arithmetic and copies ran while one was open for 13% of the time, Pallas kernels for 8%

profile of v1, /device:TPU:0, one launch (start us, length us, event | category | flops | bytes accessed | tf_op | source)
XLA Modules:
  0.0 692.7 jit_solution(12422798043852064945)
XLA Ops:
  11.6 63.3 %all-gather.5.cloned.1.call-done = bf16[768,2432]{1,0:T(8,128)(2,1)} async-done(((bf16[24,2432]{1,0:T(8,128)(2,1)}), bf16[768,2432]{1,0:T(8,128)(2,1)}) %all-gather.5.cloned.1.call-update) | async-done | bytes 3735568 | tf_op jit(solution)/shard_map/all_gather | solution.py:257
  74.9 4.2 convolution_bitcast_fusion
  84.2 3.4 collective-permute-start
  91.0 4.2 collective-permute-start.2
  96.7 3.0 pad_maximum_fusion.1
  99.6 2.5 fusion.58
  102.2 24.4 %shard_map.333 = (bf16[512,768]{1,0:T(8,128)(2,1)}, f32[6,8,512]{2,1,0:T(8,128)}) custom-call(f32[12]{0:T(128)} %constant.169.clone.slopes, bf16[512,768]{1,0:T(8,128)(2,1)} %get-tuple-element.137.q_ref, bf16[1536,768]{1,0:T(8,128)(2,1)} %get-tuple-element.135.k_ref, bf16[1536,768]{1,0:T(8,128)(2,1)} %get-tuple-element.134.v_ref, s32[1,512]{1,0:T(1,128)} %seg_ref.3, ...), custom_call_target="tpu_custom_call" | custom-call | flops 4026531840 | bytes 14155776 | tf_op jit(solution)/shard_map/pallas_call | solution.py:76
  126.6 40.3 %all-gather.7.cloned.1.call-done = bf16[768,6912]{1,0:T(8,128)(2,1)} async-done(((bf16[24,6912]{1,0:T(8,128)(2,1)}), bf16[768,6912]{1,0:T(8,128)(2,1)}) %all-gather.7.cloned.1.call-update) | async-done | bytes 10616848 | tf_op jit(solution)/shard_map/all_gather | solution.py:257
  166.9 2.4 fusion.61
  169.6 8.0 %fusion.3 = f32[512,6144]{1,0:T(8,128)S(1)} fusion(bf16[768,6912]{1,0:T(8,128)(2,1)} %all-gather.7.cloned.1.call-done, f32[512,768]{1,0:T(8,128)S(1)} %get-tuple-element.149, f32[768]{0:T(1024)S(1)} %get-tuple-element.121, f32[768]{0:T(1024)S(1)} %get-tuple-element.122, f32[512]{0:T(512)S(1)} %add_rsqrt_fusion.1, f32[512]{0:T(512)S(1)} %broadcast_multiply_fusion.5), kind=kOutput, calls=%fused_computation.6 | convolution fusion | flops 4833804288 | bytes 23603200 | tf_op jit(solution)/shard_map/dot_general | solution.py:19
  177.6 4.6 copy-done.2
  182.1 14.8 %multiply_convert_fusion.1 = (bf16[512,3072]{1,0:T(8,128)(2,1)}, f32[512,3072]{1,0:T(8,128)}) fusion(f32[512,6144]{1,0:T(8,128)S(1)} %fusion.3), kind=kLoop, calls=%fused_computation.12 | loop fusion | flops 103809024 | bytes 22020096 | tf_op jit(solution)/shard_map/convert_element_type | solution.py:317
  197.0 35.6 %all-gather.9.cloned.1.call-done = bf16[3072,768]{1,0:T(8,128)(2,1)} async-done(((bf16[96,768]{1,0:T(8,128)(2,1)}), bf16[3072,768]{1,0:T(8,128)(2,1)}) %all-gather.9.cloned.1.call-update) | async-done | bytes 4718608 | tf_op jit(solution)/shard_map/all_gather | solution.py:257
  232.5 6.6 fusion.62
  242.5 10.0 %multiply_convert_fusion = (bf16[512,3072]{1,0:T(8,128)(2,1)}, bf16[512,3072]{1,0:T(8,128)(2,1)}) fusion(f32[512,3072]{1,0:T(8,128)} %get-tuple-element.131, f32[512,6144]{1,0:T(8,128)S(1)} %copy-done.3, bf16[3072,768]{1,0:T(8,128)(2,1)} %all-gather.9.cloned.1.call-done, f32[512,768]{1,0:T(8,128)} %get-tuple-element.127), kind=kOutput, calls=%fused_computation.11 | convolution fusion | flops 2444623872 | bytes 31457280 | tf_op jit(solution)/shard_map/dot_general | solution.py:23
  252.5 10.6 %convolution_convert_fusion = bf16[768,6144]{1,0:T(8,128)(2,1)} fusion(bf16[512,3072]{1,0:T(8,128)(2,1)} %get-tuple-element.133, bf16[512,3072]{1,0:T(8,128)(2,1)} %get-tuple-element.132, f32[512,768]{1,0:T(8,128)S(1)} %copy-done.6, f32[768]{0:T(1024)S(1)} %get-tuple-element.121, f32[768]{0:T(1024)S(1)} %get-tuple-element.122, f32[512]{0:T(512)S(1)} %add_rsqrt_fusion.1, ...), kind=kOutput, calls=%fused_computation | convolution fusion | flops 4851105792 | bytes 17311744 | tf_op jit(solution)/shard_map/dot_general | solution.py:27
  263.4 11.9 %multiply_reduce_fusion = (bf16[768]{0:T(1024)(128)(2,1)S(1)}, f32[512]{0:T(512)S(1)}, f32[512]{0:T(512)S(1)}, bf16[768]{0:T(1024)(128)(2,1)S(1)}, f32[512,768]{1,0:T(8,128)S(1)}) fusion(f32[512,768]{1,0:T(8,128)S(1)} %copy-done.6, f32[512]{0:T(512)S(1)} %add_rsqrt_fusion.1, f32[512]{0:T(512)S(1)} %broadcast_multiply_fusion.5, ...), kind=kOutput, calls=%fused_computation.54 | convolution fusion | flops 4848350208 | bytes 20461568 | tf_op jit(solution)/shard_map/dot_general | solution.py:23
  275.9 3.0 convolution_convert_fusion.4.do_ref
  278.9 29.9 %shard_map.334 = (bf16[512,768]{1,0:T(8,128)(2,1)}, bf16[2,512,768]{2,1,0:T(8,128)(2,1)}, f32[2,512,768]{2,1,0:T(8,128)}, bf16[2,512,768]{2,1,0:T(8,128)(2,1)}) custom-call(f32[12]{0:T(128)} %constant.169.clone.slopes, bf16[512,768]{1,0:T(8,128)(2,1)} %get-tuple-element.137.q_ref, bf16[1536,768]{1,0:T(8,128)(2,1)} %get-tuple-element.135.k_ref, ...), custom_call_target="tpu_custom_call" | custom-call | flops 10066329600 | bytes 23592960 | tf_op jit(solution)/shard_map/pallas_call | solution.py:173
  310.1 4.5 collective-permute-start.5
  318.3 2.3 add_convert_fusion.1
  322.0 3.9 fusion.13
  325.9 2.8 fusion.12
  328.8 7.2 %convolution_convert_fusion.1 = bf16[3072,768]{1,0:T(8,128)(2,1)} fusion(bf16[512,3072]{1,0:T(8,128)(2,1)} %get-tuple-element.130, f32[512,768]{1,0:T(8,128)} %get-tuple-element.127), kind=kOutput, calls=%fused_computation.28 | convolution fusion | flops 2418671616 | bytes 9437184 | tf_op jit(solution)/shard_map/dot_general | solution.py:27
  337.9 62.9 %reduce-scatter.4.cloned.1.call-done = bf16[24,6144]{1,0:T(8,128)(2,1)} async-done(((bf16[768,6144]{1,0:T(8,128)(2,1)}), bf16[24,6144]{1,0:T(8,128)(2,1)}) %reduce-scatter.4.cloned.1.call-update) | async-done | bytes 294928 | tf_op jit(solution)/shard_map/reduce_scatter | solution.py:261
  400.8 5.7 add_bitcast_fusion
  406.5 145.6 %all-reduce.5.cloned.1.call-done = bf16[768,3200]{0,1:T(8,128)(2,1)} async-done(((bf16[768,3200]{0,1:T(8,128)(2,1)}), bf16[768,3200]{0,1:T(8,128)(2,1)}) %all-reduce.5.cloned.1.call-update) | async-done | bytes 4915216
  554.2 7.5 %all_gather.21 = bf16[96,3200]{1,0:T(8,128)(2,1)S(1)} all-gather(bf16[24,3200]{1,0:T(8,128)(2,1)S(1)} %copy.60), channel_id=1, replica_groups=mesh['ctx'=4,'fsdp'=8] {'ctx'}, dimensions={0}, use_global_device_ids=true | all-gather | bytes 768000 | tf_op jit(solution)/shard_map/all_gather | solution.py:367
  563.7 100.9 %reduce-scatter.6.cloned.1.call-done = bf16[96,768]{1,0:T(8,128)(2,1)} async-done(((bf16[3072,768]{1,0:T(8,128)(2,1)}), bf16[96,768]{1,0:T(8,128)(2,1)}) %reduce-scatter.6.cloned.1.call-update) | async-done | bytes 147472 | tf_op jit(solution)/shard_map/reduce_scatter | solution.py:261
  664.6 7.7 %all_gather.23 = bf16[384,768]{1,0:T(8,128)(2,1)S(1)} all-gather(bf16[96,768]{1,0:T(8,128)(2,1)} %reduce-scatter.6.cloned.1.call-done), channel_id=1, replica_groups=mesh['ctx'=4,'fsdp'=8] {'ctx'}, dimensions={0}, use_global_device_ids=true | all-gather | bytes 737280 | tf_op jit(solution)/shard_map/all_gather | solution.py:367
  673.3 9.4 %all-gather.11.cloned.1.call-done = bf16[96,6144]{1,0:T(8,128)(2,1)} async-done(((bf16[24,6144]{1,0:T(8,128)(2,1)}), bf16[96,6144]{1,0:T(8,128)(2,1)}) %all-gather.11.cloned.1.call-update) | async-done | bytes 1179664 | tf_op jit(solution)/shard_map/all_gather | solution.py:367
  682.7 2.9 fusion.59
  (98 shorter events, 31.3 us)
Async XLA Ops:
  7.2 81.7 %copy-start = (bf16[384,768]{1,0:T(8,128)(2,1)S(1)}, bf16[384,768]{1,0:T(8,128)(2,1)}, u32[]{:S(2)}) copy-start(bf16[384,768]{1,0:T(8,128)(2,1)} %param.37) | copy-start | bytes 1769476
  7.2 67.7 %all-gather.5.cloned.1.call-start = ((), (), s32[]{:S(2)}) async-start(), calls=%async_computation.2 | async-start | bytes 3852288 | tf_op jit(solution)/shard_map/all_gather | solution.py:257
  9.7 157.1 %all-gather.7.cloned.1.call-start = ((), (), s32[]{:S(2)}) async-start(), calls=%async_computation.3 | async-start | bytes 10948608 | tf_op jit(solution)/shard_map/all_gather | solution.py:257
  11.5 221.0 %all-gather.9.cloned.1.call-start = ((), (), s32[]{:S(2)}) async-start(), calls=%async_computation.4 | async-start | bytes 4866048 | tf_op jit(solution)/shard_map/all_gather | solution.py:257
  81.8 7.9 %copy-start.10 = (s32[1,512]{1,0:T(1,128)S(1)}, s32[1,512]{1,0:T(1,128)}, u32[]{:S(2)}) copy-start(s32[1,512]{1,0:T(1,128)} %param.30) | copy-start | bytes 6148
  81.8 7.9 %copy-start.11 = (s32[1,512]{1,0:T(1,128)S(1)}, s32[1,512]{1,0:T(1,128)}, u32[]{:S(2)}) copy-start(s32[1,512]{1,0:T(1,128)} %seg_ref.3) | copy-start | bytes 6148
  84.2 12.4 %collective-permute-start = (bf16[512,1536]{1,0:T(8,128)(2,1)}, bf16[512,1536]{1,0:T(8,128)(2,1)}, u32[]{:S(2)}, u32[]{:S(2)}) collective-permute-start(bf16[512,1536]{1,0:T(8,128)(2,1)} %pad_maximum_fusion.5), channel_id=1, source_target_pairs={{0,8},{8,16},{16,24},{1,9},{9,17},{17,25},{2,10},{10,18},{18,26},{... | collective-permute-start | bytes 4718600 | tf_op jit(solution)/shard_map/ppermute | solution.py:223
  87.6 9.0 %collective-permute-start.1 = (bf16[512,1536]{1,0:T(8,128)(2,1)}, bf16[512,1536]{1,0:T(8,128)(2,1)}, u32[]{:S(2)}, u32[]{:S(2)}) collective-permute-start(bf16[512,1536]{1,0:T(8,128)(2,1)} %pad_maximum_fusion.5), channel_id=1, source_target_pairs={{8,0},{16,8},{24,16},{9,1},{17,9},{25,17},{10,2},{18,10},{26,18},{... | collective-permute-start | bytes 4718600 | tf_op jit(solution)/shard_map/ppermute | solution.py:228
  89.6 311.2 %reduce-scatter.4.cloned.1.call-start = ((), (), s32[]{:S(2)}) async-start(), calls=%async_computation.5 | async-start | bytes 9732096 | tf_op jit(solution)/shard_map/reduce_scatter | solution.py:261
  89.7 5.5 collective-permute-start.3
  91.0 4.5 collective-permute-start.2
  102.2 64.7 %copy-start.12 = (bf16[1,512,768]{2,1,0:T(8,128)(2,1)S(1)}, bf16[1,512,768]{2,1,0:T(8,128)(2,1)}, u32[]{:S(2)}) copy-start(bf16[1,512,768]{2,1,0:T(8,128)(2,1)} %param.28) | copy-start | bytes 2359300
  169.2 8.3 %copy-start.5 = (f32[512,768]{1,0:T(8,128)}, f32[512,768]{1,0:T(8,128)S(1)}, u32[]{:S(2)}) copy-start(f32[512,768]{1,0:T(8,128)S(1)} %get-tuple-element.149) | copy-start | bytes 4718596
  177.6 4.6 copy-start.2
  232.5 6.9 %copy-start.4 = (bf16[1,512,768]{2,1,0:T(8,128)(2,1)S(1)}, bf16[1,512,768]{2,1,0:T(8,128)(2,1)}, u32[]{:S(2)}) copy-start(bf16[1,512,768]{2,1,0:T(8,128)(2,1)} %param.46) | copy-start | bytes 2359300
  232.5 10.0 %copy-start.3 = (f32[512,6144]{1,0:T(8,128)S(1)}, f32[512,6144]{1,0:T(8,128)}, u32[]{:S(2)}) copy-start(f32[512,6144]{1,0:T(8,128)} %copy-done.2) | copy-start | bytes 37748740
  242.5 10.0 %copy-start.6 = (f32[512,768]{1,0:T(8,128)S(1)}, f32[512,768]{1,0:T(8,128)}, u32[]{:S(2)}) copy-start(f32[512,768]{1,0:T(8,128)} %copy-done.5) | copy-start | bytes 4718596
  263.2 289.0 %all-reduce.5.cloned.1.call-start = ((), (), s32[]{:S(2)}) async-start(), calls=%async_computation.8 | async-start | bytes 9830400
  263.4 11.9 %copy-start.7 = (f32[512,768]{1,0:T(8,128)S(1)}, f32[512,768]{1,0:T(8,128)}, u32[]{:S(2)}) copy-start(f32[512,768]{1,0:T(8,128)} %copy-done.5) | copy-start | bytes 4718596
  308.8 9.5 %collective-permute-start.4 = (bf16[2,512,768]{2,1,0:T(8,128)(2,1)}, bf16[2,512,768]{2,1,0:T(8,128)(2,1)}, u32[]{:S(2)}, u32[]{:S(2)}) collective-permute-start(bf16[2,512,768]{2,1,0:T(8,128)(2,1)} %get-tuple-element.67), channel_id=1, source_target_pairs={{8,0},{16,8},{24,16},{9,1},{17,9},{25,17},{10,2},{18,10},{26,18},{... | collective-permute-start | bytes 4718600 | tf_op jit(solution)/shard_map/ppermute | solution.py:228
  310.1 8.2 %collective-permute-start.5 = (bf16[2,512,768]{2,1,0:T(8,128)(2,1)}, bf16[2,512,768]{2,1,0:T(8,128)(2,1)}, u32[]{:S(2)}, u32[]{:S(2)}) collective-permute-start(bf16[2,512,768]{2,1,0:T(8,128)(2,1)} %get-tuple-element.68), channel_id=1, source_target_pairs={{0,8},{8,16},{16,24},{1,9},{9,17},{17,25},{2,10},{10,18},{18,26},{... | collective-permute-start | bytes 4718600 | tf_op jit(solution)/shard_map/ppermute | solution.py:223
  316.0 2.2 copy-start.8
  328.7 335.8 %reduce-scatter.6.cloned.1.call-start = ((), (), s32[]{:S(2)}) async-start(), calls=%async_computation.7 | async-start | bytes 4866048 | tf_op jit(solution)/shard_map/reduce_scatter | solution.py:261
  336.0 0.7 copy-start.13
  336.0 64.8 %copy-start.9 = (bf16[512,768]{1,0:T(8,128)(2,1)S(1)}, bf16[512,768]{1,0:T(8,128)(2,1)}, u32[]{:S(2)}) copy-start(bf16[512,768]{1,0:T(8,128)(2,1)} %get-tuple-element.65) | copy-start | bytes 2359300
  336.1 346.6 %all-gather.11.cloned.1.call-start = ((), (), s32[]{:S(2)}) async-start(), calls=%async_computation.6 | async-start | bytes 1474560 | tf_op jit(solution)/shard_map/all_gather | solution.py:367
  562.7 122.9 %copy-start.1 = (bf16[384,768]{1,0:T(8,128)(2,1)S(1)}, bf16[384,768]{1,0:T(8,128)(2,1)}, u32[]{:S(2)}) copy-start(bf16[384,768]{1,0:T(8,128)(2,1)} %param.37) | copy-start | bytes 1769476
Sparse Core Ops, SparseCore 0:
  11.5 63.2 all-gather.4
  78.4 88.4 all-gather.6
  170.3 62.1 all-gather.8
  263.3 137.4 reduce-scatter.3
  407.3 144.7 all-reduce.4
  558.4 106.1 reduce-scatter.5
  666.1 16.5 all-gather.10

commit v2 on v1

v2 whole, which is shorter than its diff:
```python
import math
import jax
import jax.numpy as jnp
from jax import lax
from jax.experimental import pallas as pl
from jax.experimental.pallas import tpu as pltpu
from jax.sharding import PartitionSpec as P

H = 12
HD = 64
FF = 3072
HALF = 512
EPSILON = 1e-06
VECTORS = 8
QB = 256
SPAN = QB + 2 * HALF
BIG = 1e30
VMEM_LIMIT = 56 * 1024 * 1024

Z_SWAP = ((0, 1), (1, 0), (2, 3), (3, 2))
Z_MID = ((1, 2), (2, 1))
Z_OUT = ((1, 0), (2, 3))
Z_IN = ((0, 1), (3, 2))


def dot_nn(a, b):
    return lax.dot_general(a, b, (((1,), (0,)), ((), ())), preferred_element_type=jnp.float32)


def dot_nt(a, b):
    return lax.dot_general(a, b, (((1,), (1,)), ((), ())), preferred_element_type=jnp.float32)


def dot_tn(a, b):
    return lax.dot_general(a, b, (((0,), (0,)), ((), ())), preferred_element_type=jnp.float32)


def tie(*values):
    return lax.optimization_barrier(values)


def head_slopes(number):
    power_two = 2 ** int(math.floor(math.log2(number)))
    first_part = [2.0 ** (-8.0 * (position + 1) / power_two) for position in range(power_two)]
    extra_part = [
        2.0 ** (-8.0 * (2 * position + 1) / (2 * power_two))
        for position in range(number - power_two)
    ]
    return jnp.array(first_part + extra_part, dtype=jnp.float32)


def over_core(x):
    count = lax.axis_size("ctx")
    return lax.ppermute(x, "ctx", [(i, i ^ 1) for i in range(count)])


def from_previous_chip(x):
    count = lax.axis_size("ctx")
    return lax.ppermute(x, "ctx", [(i, i + 2) for i in range(count - 2)])


def from_next_chip(x):
    count = lax.axis_size("ctx")
    return lax.ppermute(x, "ctx", [(i + 2, i) for i in range(count - 2)])


def over_x(x):
    return lax.ppermute(x, "ctx", [(i, i ^ 2) for i in range(4)])


def over_y(x):
    return lax.ppermute(x, "fsdp", [(i, i ^ 1) for i in range(8)])


def over_z(x, moves):
    return lax.ppermute(
        x, "fsdp", [(2 * a + y, 2 * b + y) for a, b in moves for y in range(2)]
    )


def ordered(core, own, other, axis):
    return jnp.where(
        core == 0,
        jnp.concatenate([own, other], axis=axis),
        jnp.concatenate([other, own], axis=axis),
    )


def shard_number(k, dy):
    me = lax.axis_index("fsdp")
    return me ^ (2 * k + dy)


def place_kernel(numbers, *refs):
    pieces, out, sems = refs[:8], refs[8], refs[9]
    rows = pieces[0].shape[0]
    copies = [
        pltpu.make_async_copy(
            piece, out.at[pl.ds(pl.multiple_of(numbers[i] * rows, rows), rows), :], sems.at[i]
        )
        for i, piece in enumerate(pieces)
    ]
    for copy in copies:
        copy.start()
    for copy in copies:
        copy.wait()


def place(pieces):
    rows, width = pieces[0].shape
    numbers = jnp.stack([shard_number(k, dy) for dy in range(2) for k in range(4)])
    return pl.pallas_call(
        place_kernel,
        in_specs=[pl.BlockSpec(memory_space=pltpu.SMEM)] + [pl.BlockSpec(memory_space=pl.ANY)] * 8,
        out_specs=pl.BlockSpec(memory_space=pl.ANY),
        out_shape=jax.ShapeDtypeStruct((8 * rows, width), pieces[0].dtype),
        scratch_shapes=[pltpu.SemaphoreType.DMA((8,))],
        cost_estimate=pl.CostEstimate(
            flops=0, bytes_accessed=4 * 8 * rows * width, transcendentals=0
        ),
    )(numbers, *pieces)


class Gather:
    def __init__(self, piece):
        self.own = piece

    def first(self):
        self.y0, self.a, self.b = tie(
            over_y(self.own), over_z(self.own, Z_SWAP), over_z(self.own, Z_MID)
        )

    def second(self):
        self.c, d, self.ya = tie(
            over_z(self.a, Z_MID), over_z(self.b, Z_OUT), over_y(self.a)
        )
        self.z2 = self.c + d

    def third(self):
        e, self.yz2 = tie(over_z(self.c, Z_OUT), over_y(self.z2))
        self.z3 = self.b + e

    def fourth(self):
        self.yz3 = over_y(self.z3)

    def result(self):
        return place(
            [self.own, self.a, self.z2, self.z3, self.y0, self.ya, self.yz2, self.yz3]
        )


class Reduce:
    def __init__(self, full):
        self.full = full
        self.rows = full.shape[0] // 8

    def part(self, k, dy):
        return lax.dynamic_slice_in_dim(
            self.full, shard_number(k, dy) * self.rows, self.rows, 0
        )

    def first(self):
        self.q3 = self.part(3, 0) + over_y(self.part(3, 1))

    def second(self):
        y2, self.e = tie(over_y(self.part(2, 1)), over_z(self.q3, Z_IN))
        self.q2 = self.part(2, 0) + y2

    def third(self):
        y1, self.d, self.c = tie(
            over_y(self.part(1, 1)), over_z(self.q2, Z_IN), over_z(self.q2 + self.e, Z_MID)
        )
        self.q1 = self.part(1, 0) + y1

    def fourth(self):
        y0, b, a = tie(
            over_y(self.part(0, 1)),
            over_z(self.q3 + self.d, Z_MID),
            over_z(self.q1 + self.c, Z_SWAP),
        )
        self.total = self.part(0, 0) + y0 + a + b

    def result(self):
        return self.total


class PlainGather:
    def __init__(self, piece):
        self.own = piece

    def first(self):
        pass

    second = third = fourth = first

    def result(self):
        return lax.all_gather(self.own, "fsdp", axis=0, tiled=True)


class PlainReduce:
    def __init__(self, full):
        self.full = full

    def first(self):
        pass

    second = third = fourth = first

    def result(self):
        return lax.psum_scatter(self.full, "fsdp", scatter_dimension=0, tiled=True)


def both_cores(total, core):
    count = lax.axis_size("ctx")
    if count == 4:
        total = total + over_x(total)
        other = over_core(total)
        first = jnp.where(core == 0, total, other)
        second = jnp.where(core == 0, other, total)
        return first.astype(jnp.float32), second.astype(jnp.float32)
    slots = jnp.stack(
        [jnp.where(core == i, total, jnp.zeros_like(total)) for i in range(2)]
    )
    slots = lax.psum(slots, "ctx").astype(jnp.float32)
    return slots[0], slots[1]


def fill_distance(dist, seg_ref, tag_ref, first_row):
    for b in range(dist.shape[0]):
        base = first_row + b * QB
        key_pos = lax.broadcasted_iota(jnp.int32, (SPAN, QB), 0)
        row_pos = lax.broadcasted_iota(jnp.int32, (SPAN, QB), 1) + HALF
        gap = jnp.abs(key_pos - row_pos)
        same = tag_ref[base : base + SPAN, :] == seg_ref[:, b * QB : (b + 1) * QB]
        kept = ((gap <= HALF) & same) | (gap == 0)
        dist[b] = jnp.where(kept, gap.astype(jnp.float32), BIG)


def attn_fwd_kernel(
    first_row, slopes, q_ref, k_ref, v_ref, seg_ref, tag_ref, out_ref, lse_ref, dist
):
    rows = q_ref.shape[0]
    pair = pl.program_id(0)

    @pl.when(pair == 0)
    def _():
        fill_distance(dist, seg_ref, tag_ref, first_row)

    lane = lax.broadcasted_iota(jnp.int32, (QB, 2 * HD), 1)
    v_t = v_ref[first_row : first_row + rows + 2 * HALF, :].T
    for b in range(rows // QB):
        base = b * QB
        q = q_ref[base : base + QB, :]
        k = k_ref[first_row + base : first_row + base + SPAN, :]
        parts = []
        for a in range(2):
            mine = (lane >= HD) if a else (lane < HD)
            q_a = jnp.where(mine, q, jnp.zeros_like(q)) * jnp.asarray(1.0 / math.sqrt(HD), q.dtype)
            s = dot_nt(k, q_a) - slopes[2 * pair + a] * dist[b]
            top = jnp.max(s, axis=0, keepdims=True)
            p = jnp.exp(s - top)
            total = jnp.sum(p, axis=0, keepdims=True)
            o_t = dot_nn(v_t[a * HD : (a + 1) * HD, base : base + SPAN], p.astype(jnp.bfloat16))
            parts.append(o_t * (1.0 / total))
            lse_ref[0, a : a + 1, base : base + QB] = top + jnp.log(total)
        out_ref[base : base + QB, :] = jnp.concatenate(parts, axis=0).T.astype(jnp.bfloat16)


def attention_forward(part, queries, kv_ext, seg_row, tag_col, slopes):
    rows = HALF
    width = queries.shape[1]
    ext = kv_ext.shape[0]
    pairs = width // (2 * HD)

    def body(*refs):
        attn_fwd_kernel(part * rows, *refs)

    return pl.pallas_call(
        body,
        grid=(pairs,),
        in_specs=[
            pl.BlockSpec(memory_space=pltpu.SMEM),
            pl.BlockSpec((rows, 2 * HD), lambda h: (part, h)),
            pl.BlockSpec((ext, 2 * HD), lambda h: (0, h)),
            pl.BlockSpec((ext, 2 * HD), lambda h: (0, pairs + h)),
            pl.BlockSpec((1, rows), lambda h: (0, part)),
            pl.BlockSpec((ext, 1), lambda h: (0, 0)),
        ],
        out_specs=[
            pl.BlockSpec((rows, 2 * HD), lambda h: (0, h)),
            pl.BlockSpec((1, 8, rows), lambda h: (h, 0, 0)),
        ],
        out_shape=[
            jax.ShapeDtypeStruct((rows, width), jnp.bfloat16),
            jax.ShapeDtypeStruct((pairs, 8, rows), jnp.float32),
        ],
        scratch_shapes=[pltpu.VMEM((rows // QB, SPAN, QB), jnp.float32)],
        compiler_params=pltpu.CompilerParams(vmem_limit_bytes=VMEM_LIMIT),
        cost_estimate=pl.CostEstimate(
            flops=16 * pairs * rows * SPAN * HD,
            bytes_accessed=8 * ext * width,
            transcendentals=2 * pairs * rows * SPAN,
        ),
    )(slopes, queries, kv_ext, kv_ext, seg_row, tag_col)


def attn_bwd_kernel(
    first_row, slopes, q_ref, k_ref, v_ref, o_ref, do_ref, lse_ref, seg_ref, tag_ref,
    dq_ref, dk_ref, dv_ref, dist,
):
    rows = q_ref.shape[0]
    pair = pl.program_id(0)

    @pl.when(pair == 0)
    def _():
        fill_distance(dist, seg_ref, tag_ref, first_row)

    lane = lax.broadcasted_iota(jnp.int32, (QB, 2 * HD), 1)
    lane_one = lax.broadcasted_iota(jnp.int32, (8, 2 * HD), 1)
    k_t = k_ref[first_row : first_row + rows + 2 * HALF, :].T
    scale = 1.0 / math.sqrt(HD)
    dk_ref[...] = jnp.zeros_like(dk_ref)
    dv_ref[...] = jnp.zeros_like(dv_ref)
    for b in range(rows // QB):
        base = b * QB
        q = q_ref[base : base + QB, :] * jnp.asarray(scale, jnp.bfloat16)
        do = do_ref[base : base + QB, :]
        k = k_ref[first_row + base : first_row + base + SPAN, :]
        v = v_ref[first_row + base : first_row + base + SPAN, :]
        mixed = do.astype(jnp.float32) * o_ref[base : base + QB, :].astype(jnp.float32)
        parts = []
        ps = []
        dss = []
        qs = []
        dos = []
        for a in range(2):
            mine = (lane >= HD) if a else (lane < HD)
            mine_one = (lane_one >= HD) if a else (lane_one < HD)
            q_a = jnp.where(mine, q, jnp.zeros_like(q))
            do_a = jnp.where(mine, do, jnp.zeros_like(do))
            delta = lax.dot_general(
                mine_one.astype(jnp.float32), mixed, (((1,), (1,)), ((), ())),
                preferred_element_type=jnp.float32, precision=lax.Precision.HIGHEST,
            )[0:1]
            s = dot_nt(k, q_a) - slopes[2 * pair + a] * dist[b]
            p = jnp.exp(s - lse_ref[0, a : a + 1, base : base + QB])
            dp = dot_nt(v, do_a)
            ds = (p * (dp - delta)).astype(jnp.bfloat16)
            parts.append(dot_nn(k_t[a * HD : (a + 1) * HD, base : base + SPAN], ds) * scale)
            ps.append(p.astype(jnp.bfloat16))
            dss.append(ds)
            qs.append(q_a)
            dos.append(do_a)
        dq_ref[base : base + QB, :] = jnp.concatenate(parts, axis=0).T.astype(jnp.bfloat16)
        dk_ref[base : base + SPAN, :] += dot_nn(
            jnp.concatenate(dss, axis=1), jnp.concatenate(qs, axis=0)
        )
        dv_ref[base : base + SPAN, :] += dot_nn(
            jnp.concatenate(ps, axis=1), jnp.concatenate(dos, axis=0)
        )


def attention_backward(part, queries, kv_ext, attended, grad_attended, lse, seg_row, tag_col, slopes):
    rows = HALF
    width = queries.shape[1]
    ext = kv_ext.shape[0]
    reach = rows + 2 * HALF
    pairs = width // (2 * HD)

    def body(*refs):
        attn_bwd_kernel(part * rows, *refs)

    return pl.pallas_call(
        body,
        grid=(pairs,),
        in_specs=[
            pl.BlockSpec(memory_space=pltpu.SMEM),
            pl.BlockSpec((rows, 2 * HD), lambda h: (part, h)),
            pl.BlockSpec((ext, 2 * HD), lambda h: (0, h)),
            pl.BlockSpec((ext, 2 * HD), lambda h: (0, pairs + h)),
            pl.BlockSpec((rows, 2 * HD), lambda h: (0, h)),
            pl.BlockSpec((rows, 2 * HD), lambda h: (part, h)),
            pl.BlockSpec((1, 8, rows), lambda h: (h, 0, 0)),
            pl.BlockSpec((1, rows), lambda h: (0, part)),
            pl.BlockSpec((ext, 1), lambda h: (0, 0)),
        ],
        out_specs=[
            pl.BlockSpec((rows, 2 * HD), lambda h: (0, h)),
            pl.BlockSpec((reach, 2 * HD), lambda h: (0, h)),
            pl.BlockSpec((reach, 2 * HD), lambda h: (0, h)),
        ],
        out_shape=[
            jax.ShapeDtypeStruct((rows, width), jnp.bfloat16),
            jax.ShapeDtypeStruct((reach, width), jnp.float32),
            jax.ShapeDtypeStruct((reach, width), jnp.float32),
        ],
        scratch_shapes=[pltpu.VMEM((rows // QB, SPAN, QB), jnp.float32)],
        compiler_params=pltpu.CompilerParams(vmem_limit_bytes=VMEM_LIMIT),
        cost_estimate=pl.CostEstimate(
            flops=40 * pairs * rows * SPAN * HD,
            bytes_accessed=16 * ext * width,
            transcendentals=2 * pairs * rows * SPAN,
        ),
    )(slopes, queries, kv_ext, kv_ext, attended, grad_attended, lse, seg_row, tag_col)


def norm_parts(values, gain_vec, offset):
    centred = values - jnp.mean(values, axis=-1, keepdims=True)
    variance = jnp.mean(centred * centred, axis=-1, keepdims=True)
    inverse = lax.rsqrt(variance + EPSILON)
    normed = centred * inverse
    return (normed * gain_vec + offset, normed, inverse)


def norm_back(upstream, normed, inverse, gain_vec):
    scaled = upstream * gain_vec
    row_inner = (
        scaled
        - jnp.mean(scaled, axis=-1, keepdims=True)
        - normed * jnp.mean(scaled * normed, axis=-1, keepdims=True)
    )
    return (row_inner * inverse, jnp.sum(upstream * normed, axis=0), jnp.sum(upstream, axis=0))


def gelu_product(gate_value, up_value):
    return jax.nn.gelu(gate_value, approximate=False) * up_value


def on_device(
    tokens, segments, padding,
    w_query, w_key, w_value, w_out, w_up, w_gate, w_down,
    bias_query, bias_value, bias_out, bias_down, gain_attn, shift_attn, gain_ffn, shift_ffn,
    cotangent,
):
    tuned = lax.axis_size("ctx") == 4 and lax.axis_size("fsdp") == 8
    row_gather, row_reduce = (Gather, Reduce) if tuned else (PlainGather, PlainReduce)
    core = lax.axis_index("ctx") % 2
    inputs = tokens[0]
    rows, width = inputs.shape
    half = width // 2
    half_ff = FF // 2

    def my_columns(matrix, count):
        return lax.dynamic_slice_in_dim(matrix, core * count, count, 1)

    def my_rows(matrix):
        return lax.dynamic_slice_in_dim(matrix, core * rows, rows, 0)

    def other_rows(matrix):
        return lax.dynamic_slice_in_dim(matrix, (1 - core) * rows, rows, 0)

    vectors = jnp.stack(
        (bias_query, bias_value, bias_out, bias_down, gain_attn, shift_attn, gain_ffn, shift_ffn), axis=1
    )
    vectors = jnp.pad(vectors, ((0, 0), (0, 128 - VECTORS)))
    first_piece = jnp.concatenate(
        [my_columns(w, half) for w in (w_query, w_key, w_value)] + [vectors], axis=1
    )
    second_piece = jnp.concatenate(
        [my_columns(w_up, half_ff), my_columns(w_gate, half_ff), my_columns(w_out, half)], axis=1
    )
    shard_down = w_down.shape[0]
    down_piece = lax.dynamic_slice_in_dim(w_down, core * (shard_down // 2), shard_down // 2, 0)
    down_halves = lax.all_gather(down_piece, "fsdp", axis=0)

    first = row_gather(first_piece)
    first.first()
    first.second()
    first.third()
    if tuned:
        first.z3, second_piece = tie(first.z3, second_piece)
    first.fourth()
    second = row_gather(second_piece)
    second.first()

    own_numbers = jnp.stack((segments[0], jnp.where(padding[0] == 1, -1, segments[0])))
    numbers = ordered(core, own_numbers, over_core(own_numbers), 1)
    tags = numbers[1]
    tag_low = from_previous_chip(tags[rows:] + 2) - 2
    tag_high = from_next_chip(tags[:rows] + 2) - 2
    tag_col = jnp.concatenate([tag_low, tags, tag_high])[:, None]
    seg_row = numbers[0][None, :]
    slopes = lax.dynamic_slice_in_dim(head_slopes(H), core * (H // 2), H // 2, 0)
    inputs_all = ordered(core, inputs, over_core(inputs), 0)

    full_first = first.result()
    full_qkv = full_first[:, : 3 * half]
    vec = full_first[:, 3 * half : 3 * half + VECTORS].T.astype(jnp.float32)
    query_bias, value_bias, out_bias, down_bias, attn_gain, attn_shift, ffn_gain, ffn_shift = [
        vec[i] for i in range(VECTORS)
    ]

    def my_part(vector):
        return lax.dynamic_slice_in_dim(vector, core * half, half, 0)

    projected = dot_nn(inputs_all, full_qkv)
    queries = (projected[:, :half] + my_part(query_bias)).astype(jnp.bfloat16)
    keys_values = jnp.concatenate(
        (projected[:, half : 2 * half], projected[:, 2 * half :] + my_part(value_bias)), axis=1
    ).astype(jnp.bfloat16)
    kv_low = from_previous_chip(keys_values[rows:])
    kv_high = from_next_chip(keys_values[:rows])
    kv_ext = jnp.concatenate([kv_low, keys_values, kv_high], axis=0)

    second.second()
    attended_0, lse_0 = attention_forward(0, queries, kv_ext, seg_row, tag_col, slopes)
    attended_1, lse_1 = attention_forward(1, queries, kv_ext, seg_row, tag_col, slopes)
    second.third()
    attended_own = jnp.concatenate([attended_0, attended_1], axis=0)
    attended_all = ordered(core, attended_own, over_core(attended_own), 1)
    attended = my_rows(attended_all)
    second.fourth()

    full_second = second.result()
    full_up_gate = full_second[:, : 2 * half_ff]
    out_half = full_second[:, 2 * half_ff :]
    full_out = ordered(core, out_half, over_core(out_half), 1)
    shards = down_halves.shape[0]
    mine_down = lax.dynamic_slice_in_dim(down_halves, core * (shards // 2), shards // 2, 0)
    send_down = lax.dynamic_slice_in_dim(down_halves, (1 - core) * (shards // 2), shards // 2, 0)
    full_down = ordered(core, mine_down[:, None], over_core(send_down)[:, None], 1).reshape(
        half_ff, width
    )

    attn_branch = dot_nn(attended, full_out) + out_bias
    first_norm, first_normed, first_inverse = norm_parts(
        inputs.astype(jnp.float32) + attn_branch, attn_gain, attn_shift
    )
    own_low = first_norm.astype(jnp.bfloat16)
    normed_low = ordered(core, own_low, over_core(own_low), 0)
    up_gate = dot_nn(normed_low, full_up_gate)
    up_value = up_gate[:, :half_ff]
    gate_value = up_gate[:, half_ff:]
    hidden = gelu_product(gate_value, up_value).astype(jnp.bfloat16)
    ffn_part = dot_nn(hidden, full_down)
    ffn_branch = (
        my_rows(ffn_part)
        + over_core(other_rows(ffn_part).astype(jnp.bfloat16)).astype(jnp.float32)
        + down_bias
    )
    output_value, second_normed, second_inverse = norm_parts(
        first_norm + ffn_branch, ffn_gain, ffn_shift
    )
    layer_out = output_value.astype(jnp.bfloat16)

    upstream = cotangent[0].astype(jnp.float32)
    grad_second, grad_ffn_gain, grad_ffn_shift = norm_back(
        upstream, second_normed, second_inverse, ffn_gain
    )
    grad_down_bias = jnp.sum(grad_second, axis=0)
    own_branch = grad_second.astype(jnp.bfloat16)
    grad_branch = ordered(core, own_branch, over_core(own_branch), 0)
    grad_down = dot_tn(hidden, grad_branch).astype(jnp.bfloat16)
    grad_down = grad_down.reshape(shards // 2, 2, shard_down // 2, width)
    keep = lax.dynamic_index_in_dim(grad_down, core, 1, keepdims=False)
    send = lax.dynamic_index_in_dim(grad_down, 1 - core, 1, keepdims=False)
    grad_down = ordered(core, keep, over_core(send), 0).reshape(shards * shard_down // 2, width)
    down_total = lax.psum_scatter(grad_down, "fsdp", scatter_dimension=0, tiled=True)

    hidden_grad = dot_nt(grad_branch, full_down)
    unused_value, pullback = jax.vjp(gelu_product, gate_value, up_value)
    grad_gate, grad_up = pullback(hidden_grad)
    grad_up_gate = jnp.concatenate((grad_up, grad_gate), axis=1).astype(jnp.bfloat16)
    reduce_ffn = row_reduce(dot_tn(normed_low, grad_up_gate).astype(jnp.bfloat16))
    reduce_ffn.first()
    normed_part = dot_nt(grad_up_gate, full_up_gate)
    grad_normed = (
        grad_second
        + my_rows(normed_part)
        + over_core(other_rows(normed_part).astype(jnp.bfloat16)).astype(jnp.float32)
    )
    grad_first, grad_attn_gain, grad_attn_shift = norm_back(
        grad_normed, first_normed, first_inverse, attn_gain
    )
    grad_out_bias = jnp.sum(grad_first, axis=0)
    own_attn_low = grad_first.astype(jnp.bfloat16)
    grad_attn_low = ordered(
        core,
        my_columns(own_attn_low, half),
        over_core(lax.dynamic_slice_in_dim(own_attn_low, (1 - core) * half, half, 1)),
        0,
    )
    grad_w_out = dot_tn(attended_all, grad_attn_low)
    own_grad = dot_nt(own_attn_low, full_out).astype(jnp.bfloat16)
    grad_attended = ordered(
        core,
        my_columns(own_grad, half),
        over_core(lax.dynamic_slice_in_dim(own_grad, (1 - core) * half, half, 1)),
        0,
    )
    reduce_ffn.second()

    dq_0, dk_0, dv_0 = attention_backward(
        0, queries, kv_ext, attended_0, grad_attended, lse_0, seg_row, tag_col, slopes
    )
    dq_1, dk_1, dv_1 = attention_backward(
        1, queries, kv_ext, attended_1, grad_attended, lse_1, seg_row, tag_col, slopes
    )
    reduce_ffn.third()
    reach_0 = jnp.concatenate([dk_0, dv_0], axis=1)
    reach_1 = jnp.concatenate([dk_1, dv_1], axis=1)
    low = reach_0[:HALF].astype(jnp.bfloat16)
    high = reach_1[2 * HALF :].astype(jnp.bfloat16)
    from_next = from_next_chip(low).astype(jnp.float32)
    from_previous = from_previous_chip(high).astype(jnp.float32)
    centre = jnp.concatenate(
        [
            reach_0[HALF : 2 * HALF] + reach_1[:HALF] + from_previous,
            reach_0[2 * HALF :] + reach_1[HALF : 2 * HALF] + from_next,
        ],
        axis=0,
    ).astype(jnp.bfloat16)
    grad_qkv = jnp.concatenate((jnp.concatenate([dq_0, dq_1], axis=0), centre), axis=1)
    reduce_ffn.fourth()
    grad_w_qkv = dot_tn(inputs_all, grad_qkv)

    def spread(vector):
        return lax.dynamic_update_slice_in_dim(jnp.zeros((width,), jnp.float32), vector, core * half, 0)

    grad_query_bias = spread(jnp.sum(grad_qkv[:, :half].astype(jnp.float32), axis=0))
    grad_value_bias = spread(jnp.sum(grad_qkv[:, 2 * half :].astype(jnp.float32), axis=0))
    grad_vectors = jnp.stack(
        (
            grad_query_bias, grad_value_bias, grad_out_bias, grad_down_bias,
            grad_attn_gain, grad_attn_shift, grad_ffn_gain, grad_ffn_shift,
        ),
        axis=0,
    )
    grad_vectors = (grad_vectors + over_core(grad_vectors)).T
    grad_vectors = jnp.pad(grad_vectors, ((0, 0), (0, 128 - VECTORS)))
    last = row_reduce(
        jnp.concatenate((grad_w_qkv, grad_w_out, grad_vectors), axis=1).astype(jnp.bfloat16)
    )
    last.first()
    last.second()
    last.third()
    last.fourth()
    input_part = dot_nt(grad_qkv, full_qkv)
    grad_inputs = (
        grad_first
        + my_rows(input_part)
        + over_core(other_rows(input_part).astype(jnp.bfloat16)).astype(jnp.float32)
    )

    down_0, down_1 = both_cores(down_total, core)
    ffn_0, ffn_1 = both_cores(reduce_ffn.result(), core)
    last_0, last_1 = both_cores(last.result(), core)

    def columns(start, count, source_0, source_1):
        return jnp.concatenate(
            (source_0[:, start : start + count], source_1[:, start : start + count]), axis=1
        )

    return (
        layer_out[None],
        grad_inputs[None],
        columns(0, half, last_0, last_1),
        columns(half, half, last_0, last_1),
        columns(2 * half, half, last_0, last_1),
        columns(3 * half, half, last_0, last_1),
        columns(0, half_ff, ffn_0, ffn_1),
        columns(half_ff, half_ff, ffn_0, ffn_1),
        jnp.concatenate((down_0, down_1), axis=0),
    ) + tuple(last_0[:, 4 * half + i] for i in range(VECTORS))


def solution(mesh):
    rows_spec = P("fsdp", "ctx", None)
    in_specs = (
        (rows_spec, P("fsdp", "ctx"), P("fsdp", "ctx"))
        + (P("fsdp", None),) * 7
        + (P("fsdp"),) * VECTORS
        + (rows_spec,)
    )
    out_specs = (rows_spec, rows_spec) + (P("fsdp", None),) * 7 + (P("fsdp"),) * VECTORS
    return jax.shard_map(
        on_device, mesh=mesh, in_specs=in_specs, out_specs=out_specs, check_vma=False
    )
```

time: 697 us -> 676 us (0.970)
  waiting for transfers between devices: 458 us -> 102 us
  Pallas kernels: 54.2 us -> 286 us
  starting transfers between devices: 16.4 us -> 112 us
  other arithmetic: 37.7 us -> 58.5 us
  blocking collectives: 15.2 us -> 0 us
  matrix products: 75.7 us -> 60.9 us
  local copies, waits for them, and re-layouts: 19.7 us -> 34 us
    pallas_call x2 -> x6, Pallas kernels: 54.2 us -> 286 us  [the longest x2 224 us: place(): pl.pallas_call(place_kernel, in_specs=[pl.BlockSpec(memory_space=pltpu.SM...]
    reduce_scatter x2 -> x1, waiting for transfers between devices: 164 us -> 0.02 us  [on_device(): lax.psum_scatter(grad_down, 'fsdp', scatter_dimension=0, tiled=True)]
    all_gather x4 -> x1, waiting for transfers between devices: 149 us -> 0.01 us  [on_device(): down_halves = lax.all_gather(down_piece, 'fsdp', axis=0)]
    unnamed x8 -> x2, waiting for transfers between devices: 146 us -> 0.03 us
    ppermute x6 -> x62, waiting for transfers between devices: 0.27 us -> 101 us  [the longest x20 55.5 us: over_z(): lax.ppermute(x, 'fsdp', [(2 * a + y, 2 * b + y) for a, b in moves for y i...]
    ppermute x6 -> x62, starting transfers between devices: 15.9 us -> 112 us  [the longest x20 70.5 us: over_z(): lax.ppermute(x, 'fsdp', [(2 * a + y, 2 * b + y) for a, b in moves for y i...]
    all_gather x2 -> x0, blocking collectives: 15.2 us -> none  [whole(): return lax.all_gather(shard, 'ctx', axis=0, tiled=True).astype(jnp.float32)]
    add x1 -> x18, other arithmetic: 0.01 us -> 12.1 us  [the longest x2 2.52 us: fourth(): self.q3 + self.d]
  transfers between devices with their start and end apart: 13 -> 64, of which waited for: 8 -> 20; matrix products, arithmetic and copies ran while one was open for 13% -> 15% of each run, Pallas kernels for 8% -> 43%
where the time goes in v2:
time: 676 us; the launch traced here: 669 us
  Pallas kernels  286 us (42%)
  starting transfers between devices  112 us (17%)
  waiting for transfers between devices  102 us (15%)
  matrix products  60.9 us (9%)
  other arithmetic  58.5 us (9%)
  local copies, waits for them, and re-layouts  34 us (5%)
  between operations  16 us (2%)
    pallas_call x2, Pallas kernels, place(): pl.pallas_call(place_kernel, in_specs=[pl.BlockSpec(memory_space=pltpu.SM...  224 us
    ppermute x20, starting transfers between devices, over_z(): lax.ppermute(x, 'fsdp', [(2 * a + y, 2 * b + y) for a, b in moves for y i...  70.5 us
    ppermute x20, waiting for transfers between devices, over_z(): lax.ppermute(x, 'fsdp', [(2 * a + y, 2 * b + y) for a, b in moves for y i...  55.5 us
    pallas_call x2, Pallas kernels, attention_backward(): pl.pallas_call(body, grid=(pairs,), in_specs=[pl.BlockSpec(memory_space=p...  34.5 us
    pallas_call x2, Pallas kernels, attention_forward(): pl.pallas_call(body, grid=(pairs,), in_specs=[pl.BlockSpec(memory_space=p...  27.6 us
    dot_general x4, matrix products, dot_nt(): lax.dot_general(a, b, (((1,), (1,)), ((), ())), preferred_element_type=jn...  21.6 us
    dot_general x4, matrix products, dot_tn(): lax.dot_general(a, b, (((0,), (0,)), ((), ())), preferred_element_type=jn...  21 us
    ppermute x16, starting transfers between devices, over_y(): return lax.ppermute(x, 'fsdp', [(i, i ^ 1) for i in range(8)])  20 us
  transfers between devices with their start and end apart: 64, of which 20 were waited for; matrix products, arithmetic and copies ran while one was open for 15% of the time, Pallas kernels for 43%

profile of v2, /device:TPU:0, one launch (start us, length us, event | category | flops | bytes accessed | tf_op | source)
XLA Modules:
  0.0 669.1 jit_solution(4680695094990194490)
XLA Ops:
  23.9 21.0 %collective-permute-done.5 = bf16[96,1280]{1,0:T(8,128)(2,1)S(1)} collective-permute-done((bf16[96,1280]{1,0:T(8,128)(2,1)S(1)}, bf16[96,1280]{1,0:T(8,128)(2,1)S(1)}, u32[]{:S(2)}, u32[]{:S(2)}) %collective-permute-start.5) | collective-permute-done | bytes 245792 | tf_op jit(solution)/shard_map/ppermute | solution.py:76
  48.7 6.9 %collective-permute-done.8.refs_6_ = bf16[96,1280]{1,0:T(8,128)(2,1)S(1)} collective-permute-done((bf16[96,1280]{1,0:T(8,128)(2,1)S(1)}, bf16[96,1280]{1,0:T(8,128)(2,1)S(1)}, u32[]{:S(2)}, u32[]{:S(2)}) %collective-permute-start.8) | collective-permute-done | bytes 245792 | tf_op jit(solution)/shard_map/ppermute | solution.py:72
  59.6 4.5 collective-permute-start.13
  64.3 6.0 collective-permute-done.9.refs_7_
  70.3 5.5 collective-permute-start.17
  75.9 61.4 %shard_map.323 = bf16[768,1280]{1,0:T(8,128)(2,1)} custom-call(s32[8]{0:T(128)} %stack.104.numbers, bf16[96,1280]{1,0:T(8,128)(2,1)} %copy-done.20, bf16[96,1280]{1,0:T(8,128)(2,1)} %copy-done.40, bf16[96,1280]{1,0:T(8,128)(2,1)} %copy-done.21, bf16[96,1280]{1,0:T(8,128)(2,1)} %copy-done.22, bf16[96,1280]{1,0:T(8,128)(2,1)} %copy-done.39, ...), custom_call_target="tpu_custom_call" | custom-call | bytes 3932160 | tf_op jit(solution)/shard_map/pallas_call | solution.py:112
  139.8 4.7 fusion.30
  160.5 16.5 %collective-permute-done.20 = bf16[96,3456]{1,0:T(8,128)(2,1)S(1)} collective-permute-done((bf16[96,3456]{1,0:T(8,128)(2,1)}, bf16[96,3456]{1,0:T(8,128)(2,1)S(1)}, u32[]{:S(2)}, u32[]{:S(2)}) %collective-permute-start.20) | collective-permute-done | bytes 663584 | tf_op jit(solution)/shard_map/ppermute | solution.py:76
  186.1 13.8 %shard_map.324 = (bf16[512,384]{1,0:T(8,128)(2,1)}, f32[3,8,512]{2,1,0:T(8,128)}) custom-call(f32[6]{0:T(128)} %dynamic_slice.124.refs_0_, bf16[1024,384]{1,0:T(8,128)(2,1)} %get-tuple-element.149.refs_1_, bf16[2048,768]{1,0:T(8,128)(2,1)} %pad_maximum_fusion.3.refs_2_.refs_3_, bf16[2048,768]{1,0:T(8,128)(2,1)} %pad_maximum_fusion.3.refs_2_.refs_3_, ...), custom_call_target="tpu_custom_call" | custom-call | flops 2013265920 | bytes 6291456 | tf_op jit(solution)/shard_map/pallas_call | solution.py:278
  203.5 13.8 %shard_map.325 = (bf16[512,384]{1,0:T(8,128)(2,1)}, f32[3,8,512]{2,1,0:T(8,128)}) custom-call(f32[6]{0:T(128)} %dynamic_slice.124.refs_0_, bf16[1024,384]{1,0:T(8,128)(2,1)} %get-tuple-element.149.refs_1_, bf16[2048,768]{1,0:T(8,128)(2,1)} %pad_maximum_fusion.3.refs_2_.refs_3_, bf16[2048,768]{1,0:T(8,128)(2,1)} %pad_maximum_fusion.3.refs_2_.refs_3_, ...), custom_call_target="tpu_custom_call" | custom-call | flops 2013265920 | bytes 6291456 | tf_op jit(solution)/shard_map/pallas_call | solution.py:278
  219.4 162.6 %shard_map.326 = bf16[768,3456]{1,0:T(8,128)(2,1)} custom-call(s32[8]{0:T(128)} %stack.104.numbers, bf16[96,3456]{1,0:T(8,128)(2,1)} %copy-done.7, bf16[96,3456]{1,0:T(8,128)(2,1)} %collective-permute-done.17.refs_1_, bf16[96,3456]{1,0:T(8,128)(2,1)} %copy-done.8, bf16[96,3456]{1,0:T(8,128)(2,1)} %copy-done.9, bf16[96,3456]{1,0:T(8,128)(2,1)} %copy-done.27, ...), custom_call_target="tpu_custom_call" | custom-call | bytes 10616832 | tf_op jit(solution)/shard_map/pallas_call | solution.py:112
  391.8 8.6 %fusion.10 = f32[1024,3072]{1,0:T(8,128)S(1)} fusion(bf16[768,3456]{1,0:T(8,128)(2,1)} %shard_map.326, bf16[512,768]{1,0:T(8,128)(2,1)} %collective-permute-done.26, bf16[512,768]{1,0:T(8,128)(2,1)S(1)} %fusion.32, pred[]{:T(512)S(6)} %eq.9), kind=kOutput, calls=%fused_computation.26 | convolution fusion | flops 4838916096 | bytes 18874368 | tf_op jit(solution)/shard_map/dot_general | solution.py:27
  400.3 15.0 %multiply_convert_fusion.1 = (bf16[1024,1536]{1,0:T(8,128)(2,1)S(1)}, f32[1024,1536]{1,0:T(8,128)}) fusion(f32[1024,3072]{1,0:T(8,128)S(1)} %fusion.10), kind=kLoop, calls=%fused_computation.5 | loop fusion | flops 103809024 | bytes 22020096 | tf_op jit(solution)/shard_map/convert_element_type | solution.py:534
  429.3 11.1 %multiply_convert_fusion = (bf16[1024,1536]{1,0:T(8,128)(2,1)S(1)}, bf16[1024,1536]{1,0:T(8,128)(2,1)S(1)}) fusion(f32[1024,1536]{1,0:T(8,128)} %get-tuple-element.138, f32[1024,3072]{1,0:T(8,128)} %copy-done.2, bf16[1536,768]{1,0:T(8,128)(2,1)} %bitcast.71, bf16[512,768]{1,0:T(8,128)(2,1)} %collective-permute-done.29, ...), kind=kOutput, calls=%fused_computation.4 | convolution fusion | flops 2451308544 | bytes 29097984 | tf_op jit(solution)/shard_map/dot_general | solution.py:31
  440.4 7.5 %fusion.8 = f32[1024,768]{1,0:T(8,128)S(1)} fusion(bf16[768,3456]{1,0:T(8,128)(2,1)} %shard_map.326, bf16[1024,1536]{1,0:T(8,128)(2,1)S(1)} %get-tuple-element.140, bf16[1024,1536]{1,0:T(8,128)(2,1)S(1)} %get-tuple-element.139), kind=kOutput, calls=%fused_computation.24 | convolution fusion | flops 4844421120 | bytes 14155776 | tf_op jit(solution)/shard_map/dot_general | solution.py:31
  447.9 7.2 %convolution_convert_fusion = bf16[768,3072]{1,0:T(8,128)(2,1)S(1)} fusion(bf16[1024,1536]{1,0:T(8,128)(2,1)S(1)} %get-tuple-element.140, bf16[1024,1536]{1,0:T(8,128)(2,1)S(1)} %get-tuple-element.139, bf16[512,768]{1,0:T(8,128)(2,1)} %collective-permute-done.26, bf16[512,768]{1,0:T(8,128)(2,1)S(1)} %copy-done.24, pred[]{:T(512)S(6)} %eq.9), kind=kOutput, calls=%fused_computation.23 | convolution fusion | flops 4853858304 | bytes 12582913 | tf_op jit(solution)/shard_map/dot_general | solution.py:35
  458.9 5.0 convolution_convert_fusion.1
  465.5 6.7 %collective-permute-done.49 = bf16[96,3072]{1,0:T(8,128)(2,1)S(1)} collective-permute-done((bf16[96,3072]{1,0:T(8,128)(2,1)S(1)}, bf16[96,3072]{1,0:T(8,128)(2,1)S(1)}, u32[]{:S(2)}, u32[]{:S(2)}) %collective-permute-start.49) | collective-permute-done | bytes 589856 | tf_op jit(solution)/shard_map/ppermute | solution.py:72
  473.2 6.2 collective-permute-start.52
  493.5 4.4 collective-permute-start.53
  500.2 17.3 %shard_map.327 = (bf16[512,384]{1,0:T(8,128)(2,1)}, f32[1536,384]{1,0:T(8,128)}, f32[1536,384]{1,0:T(8,128)}) custom-call(f32[6]{0:T(128)} %dynamic_slice.124.refs_0_, bf16[1024,384]{1,0:T(8,128)(2,1)} %get-tuple-element.149.refs_1_, bf16[2048,768]{1,0:T(8,128)(2,1)} %pad_maximum_fusion.3.refs_2_.refs_3_, ...), custom_call_target="tpu_custom_call" | custom-call | flops 5033164800 | bytes 12582912 | tf_op jit(solution)/shard_map/pallas_call | solution.py:373
  517.5 17.2 %shard_map.328 = (bf16[512,384]{1,0:T(8,128)(2,1)}, f32[1536,384]{1,0:T(8,128)}, f32[1536,384]{1,0:T(8,128)}) custom-call(f32[6]{0:T(128)} %dynamic_slice.124.refs_0_, bf16[1024,384]{1,0:T(8,128)(2,1)} %get-tuple-element.149.refs_1_, bf16[2048,768]{1,0:T(8,128)(2,1)} %pad_maximum_fusion.3.refs_2_.refs_3_, ...), custom_call_target="tpu_custom_call" | custom-call | flops 5033164800 | bytes 12582912 | tf_op jit(solution)/shard_map/pallas_call | solution.py:373
  540.1 5.0 collective-permute-start.32
  560.5 5.8 convolution_convert_fusion.2
  572.4 17.6 %collective-permute-start.56 = (bf16[96,3072]{1,0:T(8,128)(2,1)S(1)}, bf16[96,3072]{1,0:T(8,128)(2,1)S(1)}, u32[]{:S(2)}, u32[]{:S(2)}) collective-permute-start(bf16[96,3072]{1,0:T(8,128)(2,1)S(1)} %get-tuple-element.143), channel_id=1, source_target_pairs={{0,2},{1,3},{2,0},{3,1},{4,6},{5,7},{6,4},{7,5},{8,10},{9,11},{10,... | collective-permute-start | bytes 1769480 | tf_op jit(solution)/shard_map/ppermute | solution.py:76
  590.5 8.2 %collective-permute-start.41 = (bf16[96,1664]{1,0:T(8,128)(2,1)S(1)}, bf16[96,1664]{1,0:T(8,128)(2,1)S(1)}, u32[]{:S(2)}, u32[]{:S(2)}) collective-permute-start(bf16[96,1664]{1,0:T(8,128)(2,1)S(1)} %dynamic-slice_add_fusion.3), channel_id=1, source_target_pairs={{0,2},{1,3},{6,4},{7,5},{8,10},{9,11},{14,12},{15,13},{16,18},{17,... | collective-permute-start | bytes 958472 | tf_op jit(solution)/shard_map/ppermute | solution.py:76
  603.7 5.8 collective-permute-done.41
  610.2 8.0 %collective-permute-start.42 = (bf16[96,1664]{1,0:T(8,128)(2,1)S(1)}, bf16[96,1664]{1,0:T(8,128)(2,1)S(1)}, u32[]{:S(2)}, u32[]{:S(2)}) collective-permute-start(bf16[96,1664]{1,0:T(8,128)(2,1)S(1)} %get-tuple-element.129), channel_id=1, source_target_pairs={{0,2},{1,3},{6,4},{7,5},{8,10},{9,11},{14,12},{15,13},{16,18},{17,... | collective-permute-start | bytes 958472 | tf_op jit(solution)/shard_map/ppermute | solution.py:76
  620.6 4.0 collective-permute-done.42
  627.3 5.3 collective-permute-start.45
  640.3 6.6 collective-permute-done.46
  650.7 7.5 %collective-permute-done.60 = bf16[192,768]{1,0:T(8,128)(2,1)S(1)} collective-permute-done((bf16[192,768]{1,0:T(8,128)(2,1)}, bf16[192,768]{1,0:T(8,128)(2,1)S(1)}, u32[]{:S(2)}, u32[]{:S(2)}) %collective-permute-start.60) | collective-permute-done | bytes 294944 | tf_op jit(solution)/shard_map/ppermute | solution.py:68
  (347 shorter events, 156.4 us)
Async XLA Ops:
  7.2 382.5 %all-gather.3.cloned.1.call-start = ((), (), s32[]{:S(2)}) async-start(), calls=%async_computation.2 | async-start | bytes 2654208 | tf_op jit(solution)/shard_map/all_gather | solution.py:464
  16.3 122.0 %collective-permute-start = (bf16[512,768]{1,0:T(8,128)(2,1)}, bf16[512,768]{1,0:T(8,128)(2,1)}, u32[]{:S(2)}, u32[]{:S(2)}) collective-permute-start(bf16[512,768]{1,0:T(8,128)(2,1)} %bitcast.85), channel_id=1, source_target_pairs={{0,8},{8,0},{16,24},{24,16},{1,9},{9,1},{17,25},{25,17},{2,10},{10... | collective-permute-start | bytes 2359304 | tf_op jit(solution)/shard_map/ppermute | solution.py:54
  17.8 40.5 %collective-permute-start.12 = (s32[2,512]{1,0:T(2,128)S(1)}, s32[2,512]{1,0:T(2,128)S(1)}, u32[]{:S(2)}, u32[]{:S(2)}) collective-permute-start(s32[2,512]{1,0:T(2,128)S(1)} %pad_add_fusion.1), channel_id=1, source_target_pairs={{0,8},{8,0},{16,24},{24,16},{1,9},{9,1},{17,25},{25,17},{2,10},{10... | collective-permute-start | bytes 12296 | tf_op jit(solution)/shard_map/ppermute | solution.py:54
  19.0 629.8 %reduce-scatter.2.cloned.1.call-start = ((), (), s32[]{:S(2)}) async-start(), calls=%async_computation.1 | async-start | bytes 2654208 | tf_op jit(solution)/shard_map/reduce_scatter | solution.py:558
  22.1 22.8 %collective-permute-start.6 = (bf16[96,1280]{1,0:T(8,128)(2,1)S(1)}, bf16[96,1280]{1,0:T(8,128)(2,1)S(1)}, u32[]{:S(2)}, u32[]{:S(2)}) collective-permute-start(bf16[96,1280]{1,0:T(8,128)(2,1)S(1)} %collective-permute-done.2.refs_1_), channel_id=1, source_target_pairs={{0,1},{1,0},{2,3},{3,2},{4,5},{5,4},{6,7},{7,6},{8,9},{9,8},{10,11... | collective-permute-start | bytes 737288 | tf_op jit(solution)/shard_map/ppermute | solution.py:72
  22.6 22.4 %collective-permute-start.5 = (bf16[96,1280]{1,0:T(8,128)(2,1)S(1)}, bf16[96,1280]{1,0:T(8,128)(2,1)S(1)}, u32[]{:S(2)}, u32[]{:S(2)}) collective-permute-start(bf16[96,1280]{1,0:T(8,128)(2,1)S(1)} %collective-permute-done.3), channel_id=1, source_target_pairs={{2,0},{3,1},{4,6},{5,7},{10,8},{11,9},{12,14},{13,15},{18,16},{19,... | collective-permute-start | bytes 737288 | tf_op jit(solution)/shard_map/ppermute | solution.py:76
  58.3 98.2 %collective-permute-start.14 = (s32[512]{0:T(512)S(1)}, s32[512]{0:T(512)S(1)}, u32[]{:S(2)}, u32[]{:S(2)}) collective-permute-start(s32[512]{0:T(512)S(1)} %bitcast.76), channel_id=1, source_target_pairs={{16,0},{24,8},{17,1},{25,9},{18,2},{26,10},{19,3},{27,11},{20,4},{... | collective-permute-start | bytes 6152 | tf_op jit(solution)/shard_map/ppermute | solution.py:64
  59.6 98.9 %collective-permute-start.13 = (s32[512]{0:T(512)S(1)}, s32[512]{0:T(512)S(1)}, u32[]{:S(2)}, u32[]{:S(2)}) collective-permute-start(s32[512]{0:T(512)S(1)} %bitcast.75), channel_id=1, source_target_pairs={{0,16},{8,24},{1,17},{9,25},{2,18},{10,26},{3,19},{11,27},{4,20},{... | collective-permute-start | bytes 6152 | tf_op jit(solution)/shard_map/ppermute | solution.py:59
  64.2 84.5 %collective-permute-start.16 = (bf16[96,3456]{1,0:T(8,128)(2,1)S(1)}, bf16[96,3456]{1,0:T(8,128)(2,1)S(1)}, u32[]{:S(2)}, u32[]{:S(2)}) collective-permute-start(bf16[96,3456]{1,0:T(8,128)(2,1)S(1)} %pad_maximum_fusion.8.refs_0_), channel_id=1, source_target_pairs={{0,1},{1,0},{2,3},{3,2},{4,5},{5,4},{6,7},{7,6},{8,9},{9,8},{10,11... | collective-permute-start | bytes 1990664 | tf_op jit(solution)/shard_map/ppermute | solution.py:72
  70.3 82.7 %collective-permute-start.17 = (bf16[96,3456]{1,0:T(8,128)(2,1)S(1)}, bf16[96,3456]{1,0:T(8,128)(2,1)}, u32[]{:S(2)}, u32[]{:S(2)}) collective-permute-start(bf16[96,3456]{1,0:T(8,128)(2,1)S(1)} %pad_maximum_fusion.8.refs_0_), channel_id=1, source_target_pairs={{0,2},{1,3},{2,0},{3,1},{4,6},{5,7},{6,4},{7,5},{8,10},{9,11},{10,... | collective-permute-start | bytes 1990664 | tf_op jit(solution)/shard_map/ppermute | solution.py:76
  149.5 33.5 %collective-permute-start.10 = (bf16[512,768]{1,0:T(8,128)(2,1)}, bf16[512,768]{1,0:T(8,128)(2,1)S(1)}, u32[]{:S(2)}, u32[]{:S(2)}) collective-permute-start(bf16[512,768]{1,0:T(8,128)(2,1)} %get-tuple-element.160), channel_id=1, source_target_pairs={{0,16},{8,24},{1,17},{9,25},{2,18},{10,26},{3,19},{11,27},{4,20},{... | collective-permute-start | bytes 2359304 | tf_op jit(solution)/shard_map/ppermute | solution.py:59
  153.0 30.0 %collective-permute-start.11 = (bf16[512,768]{1,0:T(8,128)(2,1)}, bf16[512,768]{1,0:T(8,128)(2,1)}, u32[]{:S(2)}, u32[]{:S(2)}) collective-permute-start(bf16[512,768]{1,0:T(8,128)(2,1)} %get-tuple-element.161), channel_id=1, source_target_pairs={{16,0},{24,8},{17,1},{25,9},{18,2},{26,10},{19,3},{27,11},{20,4},{... | collective-permute-start | bytes 2359304 | tf_op jit(solution)/shard_map/ppermute | solution.py:64
  156.5 20.4 %collective-permute-start.21 = (bf16[96,3456]{1,0:T(8,128)(2,1)}, bf16[96,3456]{1,0:T(8,128)(2,1)S(1)}, u32[]{:S(2)}, u32[]{:S(2)}) collective-permute-start(bf16[96,3456]{1,0:T(8,128)(2,1)} %collective-permute-done.17.refs_1_), channel_id=1, source_target_pairs={{0,1},{1,0},{2,3},{3,2},{4,5},{5,4},{6,7},{7,6},{8,9},{9,8},{10,11... | collective-permute-start | bytes 1990664 | tf_op jit(solution)/shard_map/ppermute | solution.py:72
  158.6 18.4 %collective-permute-start.20 = (bf16[96,3456]{1,0:T(8,128)(2,1)}, bf16[96,3456]{1,0:T(8,128)(2,1)S(1)}, u32[]{:S(2)}, u32[]{:S(2)}) collective-permute-start(bf16[96,3456]{1,0:T(8,128)(2,1)} %collective-permute-done.18), channel_id=1, source_target_pairs={{2,0},{3,1},{4,6},{5,7},{10,8},{11,9},{12,14},{13,15},{18,16},{19,... | collective-permute-start | bytes 1990664 | tf_op jit(solution)/shard_map/ppermute | solution.py:76
  177.8 23.1 %collective-permute-start.22 = (bf16[96,3456]{1,0:T(8,128)(2,1)}, bf16[96,3456]{1,0:T(8,128)(2,1)}, u32[]{:S(2)}, u32[]{:S(2)}) collective-permute-start(bf16[96,3456]{1,0:T(8,128)(2,1)} %collective-permute-done.19), channel_id=1, source_target_pairs={{2,0},{3,1},{4,6},{5,7},{10,8},{11,9},{12,14},{13,15},{18,16},{19,... | collective-permute-start | bytes 1990664 | tf_op jit(solution)/shard_map/ppermute | solution.py:76
  180.6 20.4 %collective-permute-start.23 = (bf16[96,3456]{1,0:T(8,128)(2,1)S(1)}, bf16[96,3456]{1,0:T(8,128)(2,1)}, u32[]{:S(2)}, u32[]{:S(2)}) collective-permute-start(bf16[96,3456]{1,0:T(8,128)(2,1)S(1)} %add.311.refs_2_), channel_id=1, source_target_pairs={{0,1},{1,0},{2,3},{3,2},{4,5},{5,4},{6,7},{7,6},{8,9},{9,8},{10,11... | collective-permute-start | bytes 1990664 | tf_op jit(solution)/shard_map/ppermute | solution.py:72
  218.4 165.3 %collective-permute-start.15 = (bf16[1024,384]{1,0:T(8,128)(2,1)S(1)}, bf16[1024,384]{1,0:T(8,128)(2,1)S(1)}, u32[]{:S(2)}, u32[]{:S(2)}) collective-permute-start(bf16[1024,384]{1,0:T(8,128)(2,1)S(1)} %constant_dynamic-update-slice_fusion), channel_id=1, source_target_pairs={{0,8},{8,0},{16,24},{24,16},{1,9},{9,1},{17,25},{25,17},{2,10},{10... | collective-permute-start | bytes 2359304 | tf_op jit(solution)/shard_map/ppermute | solution.py:54
  391.5 23.8 %collective-permute-start.27 = (bf16[4,192,768]{2,1,0:T(8,128)(2,1)S(1)}, bf16[4,192,768]{2,1,0:T(8,128)(2,1)S(1)}, u32[]{:S(2)}, u32[]{:S(2)}) collective-permute-start(bf16[4,192,768]{2,1,0:T(8,128)(2,1)S(1)} %get-tuple-element.158), channel_id=1, source_target_pairs={{0,8},{8,0},{16,24},{24,16},{1,9},{9,1},{17,25},{25,17},{2,10},{10... | collective-permute-start | bytes 3538952 | tf_op jit(solution)/shard_map/ppermute | solution.py:54
  457.1 22.3 %collective-permute-start.30 = (bf16[512,768]{1,0:T(8,128)(2,1)S(1)}, bf16[512,768]{1,0:T(8,128)(2,1)S(1)}, u32[]{:S(2)}, u32[]{:S(2)}) collective-permute-start(bf16[512,768]{1,0:T(8,128)(2,1)S(1)} %dynamic-slice_convert_fusion.1), channel_id=1, source_target_pairs={{0,8},{8,0},{16,24},{24,16},{1,9},{9,1},{17,25},{25,17},{2,10},{10... | collective-permute-start | bytes 2359304 | tf_op jit(solution)/shard_map/ppermute | solution.py:54
  464.1 22.3 %collective-permute-start.59 = (bf16[4,192,768]{2,1,0:T(8,128)(2,1)S(1)}, bf16[4,192,768]{2,1,0:T(8,128)(2,1)S(1)}, u32[]{:S(2)}, u32[]{:S(2)}) collective-permute-start(bf16[4,192,768]{2,1,0:T(8,128)(2,1)S(1)} %get-tuple-element.156), channel_id=1, source_target_pairs={{0,8},{8,0},{16,24},{24,16},{1,9},{9,1},{17,25},{25,17},{2,10},{10... | collective-permute-start | bytes 3538952 | tf_op jit(solution)/shard_map/ppermute | solution.py:54
  464.5 23.5 %collective-permute-start.51 = (bf16[96,3072]{1,0:T(8,128)(2,1)}, bf16[96,3072]{1,0:T(8,128)(2,1)}, u32[]{:S(2)}, u32[]{:S(2)}) collective-permute-start(bf16[96,3072]{1,0:T(8,128)(2,1)} %get-tuple-element.146), channel_id=1, source_target_pairs={{0,1},{1,0},{2,3},{3,2},{4,5},{5,4},{6,7},{7,6},{8,9},{9,8},{10,11... | collective-permute-start | bytes 1769480 | tf_op jit(solution)/shard_map/ppermute | solution.py:72
  484.7 60.5 %collective-permute-start.35 = (bf16[512,384]{1,0:T(8,128)(2,1)}, bf16[512,384]{1,0:T(8,128)(2,1)}, u32[]{:S(2)}, u32[]{:S(2)}) collective-permute-start(bf16[512,384]{1,0:T(8,128)(2,1)} %get-tuple-element.169), channel_id=1, source_target_pairs={{0,8},{8,0},{16,24},{24,16},{1,9},{9,1},{17,25},{25,17},{2,10},{10... | collective-permute-start | bytes 1179656 | tf_op jit(solution)/shard_map/ppermute | solution.py:54
  492.4 57.7 %collective-permute-start.50 = (bf16[96,3072]{1,0:T(8,128)(2,1)S(1)}, bf16[96,3072]{1,0:T(8,128)(2,1)S(1)}, u32[]{:S(2)}, u32[]{:S(2)}) collective-permute-start(bf16[96,3072]{1,0:T(8,128)(2,1)S(1)} %get-tuple-element.145), channel_id=1, source_target_pairs={{0,1},{1,0},{2,3},{3,2},{4,5},{5,4},{6,7},{7,6},{8,9},{9,8},{10,11... | collective-permute-start | bytes 1769480 | tf_op jit(solution)/shard_map/ppermute | solution.py:72
  493.5 56.6 %collective-permute-start.53 = (bf16[96,3072]{1,0:T(8,128)(2,1)S(1)}, bf16[96,3072]{1,0:T(8,128)(2,1)S(1)}, u32[]{:S(2)}, u32[]{:S(2)}) collective-permute-start(bf16[96,3072]{1,0:T(8,128)(2,1)S(1)} %get-tuple-element.127), channel_id=1, source_target_pairs={{0,2},{1,3},{6,4},{7,5},{8,10},{9,11},{14,12},{15,13},{16,18},{17,... | collective-permute-start | bytes 1769480 | tf_op jit(solution)/shard_map/ppermute | solution.py:76
  536.7 19.5 %collective-permute-start.33 = (bf16[512,768]{1,0:T(8,128)(2,1)S(1)}, bf16[512,768]{1,0:T(8,128)(2,1)S(1)}, u32[]{:S(2)}, u32[]{:S(2)}) collective-permute-start(bf16[512,768]{1,0:T(8,128)(2,1)S(1)} %slice.324), channel_id=1, source_target_pairs={{16,0},{24,8},{17,1},{25,9},{18,2},{26,10},{19,3},{27,11},{20,4},{... | collective-permute-start | bytes 2359304 | tf_op jit(solution)/shard_map/ppermute | solution.py:64
  540.1 19.4 %collective-permute-start.32 = (bf16[512,768]{1,0:T(8,128)(2,1)S(1)}, bf16[512,768]{1,0:T(8,128)(2,1)S(1)}, u32[]{:S(2)}, u32[]{:S(2)}) collective-permute-start(bf16[512,768]{1,0:T(8,128)(2,1)S(1)} %slice.325), channel_id=1, source_target_pairs={{0,16},{8,24},{1,17},{9,25},{2,18},{10,26},{3,19},{11,27},{4,20},{... | collective-permute-start | bytes 2359304 | tf_op jit(solution)/shard_map/ppermute | solution.py:59
  552.6 48.5 %collective-permute-start.55 = (bf16[96,3072]{1,0:T(8,128)(2,1)}, bf16[96,3072]{1,0:T(8,128)(2,1)}, u32[]{:S(2)}, u32[]{:S(2)}) collective-permute-start(bf16[96,3072]{1,0:T(8,128)(2,1)} %add.365), channel_id=1, source_target_pairs={{2,4},{3,5},{4,2},{5,3},{10,12},{11,13},{12,10},{13,11},{18,20},{1... | collective-permute-start | bytes 1769480 | tf_op jit(solution)/shard_map/ppermute | solution.py:76
  568.5 21.9 %collective-permute-start.38 = (bf16[96,1664]{1,0:T(8,128)(2,1)S(1)}, bf16[96,1664]{1,0:T(8,128)(2,1)S(1)}, u32[]{:S(2)}, u32[]{:S(2)}) collective-permute-start(bf16[96,1664]{1,0:T(8,128)(2,1)S(1)} %get-tuple-element.154), channel_id=1, source_target_pairs={{0,1},{1,0},{2,3},{3,2},{4,5},{5,4},{6,7},{7,6},{8,9},{9,8},{10,11... | collective-permute-start | bytes 958472 | tf_op jit(solution)/shard_map/ppermute | solution.py:72
  571.7 29.5 %collective-permute-start.48 = (bf16[96,3072]{1,0:T(8,128)(2,1)S(1)}, bf16[96,3072]{1,0:T(8,128)(2,1)S(1)}, u32[]{:S(2)}, u32[]{:S(2)}) collective-permute-start(bf16[96,3072]{1,0:T(8,128)(2,1)S(1)} %get-tuple-element.144), channel_id=1, source_target_pairs={{0,1},{1,0},{2,3},{3,2},{4,5},{5,4},{6,7},{7,6},{8,9},{9,8},{10,11... | collective-permute-start | bytes 1769480 | tf_op jit(solution)/shard_map/ppermute | solution.py:72
  572.4 31.3 %collective-permute-start.56 = (bf16[96,3072]{1,0:T(8,128)(2,1)S(1)}, bf16[96,3072]{1,0:T(8,128)(2,1)S(1)}, u32[]{:S(2)}, u32[]{:S(2)}) collective-permute-start(bf16[96,3072]{1,0:T(8,128)(2,1)S(1)} %get-tuple-element.143), channel_id=1, source_target_pairs={{0,2},{1,3},{2,0},{3,1},{4,6},{5,7},{6,4},{7,5},{8,10},{9,11},{10,... | collective-permute-start | bytes 1769480 | tf_op jit(solution)/shard_map/ppermute | solution.py:76
  590.5 19.0 %collective-permute-start.41 = (bf16[96,1664]{1,0:T(8,128)(2,1)S(1)}, bf16[96,1664]{1,0:T(8,128)(2,1)S(1)}, u32[]{:S(2)}, u32[]{:S(2)}) collective-permute-start(bf16[96,1664]{1,0:T(8,128)(2,1)S(1)} %dynamic-slice_add_fusion.3), channel_id=1, source_target_pairs={{0,2},{1,3},{6,4},{7,5},{8,10},{9,11},{14,12},{15,13},{16,18},{17,... | collective-permute-start | bytes 958472 | tf_op jit(solution)/shard_map/ppermute | solution.py:76
  601.1 34.2 %collective-permute-start.34 = (bf16[512,768]{1,0:T(8,128)(2,1)S(1)}, bf16[512,768]{1,0:T(8,128)(2,1)S(1)}, u32[]{:S(2)}, u32[]{:S(2)}) collective-permute-start(bf16[512,768]{1,0:T(8,128)(2,1)S(1)} %dynamic-slice_convert_fusion), channel_id=1, source_target_pairs={{0,8},{8,0},{16,24},{24,16},{1,9},{9,1},{17,25},{25,17},{2,10},{10... | collective-permute-start | bytes 2359304 | tf_op jit(solution)/shard_map/ppermute | solution.py:54
  (86 other events, 1150.8 us)
Sparse Core Ops, SparseCore 0:
  19.1 67.9 all-gather.2
  488.1 81.3 reduce-scatter.1
